TPU v7x, 512 devices: a whole 4x4x16 slice. The times are simulated.
512 devices in a mesh: reg: 32 (over z, core), lon: 16 (over y, x).
Axes of the slice: x: 4, y: 4, z: 16, core: 2. Of those that a mesh axis runs over, the one named last changes fastest.
Arguments:
- nodes: bfloat16 [1, 65536, 512], P(None, ('reg', 'lon')), may hold values from -6 to 6
- norm_gain: float32 [512], replicated, may hold values from 0.25 to 1.75
- w_qkv: bfloat16 [512, 1536], replicated
- w_out: bfloat16 [512, 512], replicated, may hold values from -0.25 to 0.25
- w_latent: bfloat16 [512, 512], replicated, may hold values from -0.25 to 0.25
- neighbours: int32 [512, 5], P(('reg', 'lon')), may hold values from 0 to 511, as said below
- assignment: int32 [64, 4096], P('reg', 'lon'), may hold values from 0 to 65535, as said below
- psi: float32 [9, 64, 5, 5], P(None, 'reg'), may hold values from -1.2 to 1.2
- w_dec: bfloat16 [9, 512, 84], replicated, may hold values from -0.09375 to 0.09375
Outputs:
- mesh_state: bfloat16 [1, 65536, 512], P(None, ('reg', 'lon'))
- fields: bfloat16 [1, 84, 64, 4096], P(None, None, 'reg', 'lon')
Inputs may be any that keep to these rules, and one draw needn't show every extreme that they name: neighbours[b, 0] = b; the other entries of a row are distinct blocks adjacent to b (diagonals included) on the grid of 32 x 16 blocks, where block b has row b // 16 and column b % 16; columns wrap around, rows do not. `assignment`: the node of cell (i, j) lies in block (i // 2) * 16 + j // 256.
All inputs are finite; a program needn't handle non-finite values.
Results may differ from a plain program's by a relative error of at most 0.011.
Values may be sent and summed in bfloat16 or wider, within the bound.
A program may use at most 64 MiB of HBM per device.

v0:
```python
import jax
import jax.numpy as jnp
from jax import lax
from jax.sharding import PartitionSpec as P

HEADS = 16


def with_halo(array, sides, width, wrap):
    for axis, dim in sides:
        size, length = (lax.axis_size(axis), array.shape[dim])
        up = [(i, (i + 1) % size) for i in range(size if wrap else size - 1)]
        down = [(j, i) for i, j in up]
        last = lax.slice_in_dim(array, length - width, length, axis=dim)
        leading = lax.slice_in_dim(array, 0, width, axis=dim)
        before = lax.ppermute(last, axis, up)
        after = lax.ppermute(leading, axis, down)
        array = jnp.concatenate([before, array, after], axis=dim)
    return array


def layer_norm(nodes, gain):
    values = nodes.astype(jnp.float32)
    center = values - jnp.mean(values, axis=-1, keepdims=True)
    spread = jnp.mean(center * center, axis=-1, keepdims=True)
    return (center * lax.rsqrt(spread + 1e-05) * gain).astype(jnp.bfloat16)


def apply_taps(extended, psi, lat_rows, lon_cols, basis_count, out_ch):
    members = extended.shape[0]
    ext_rows = extended.shape[2]
    ext_cols = extended.shape[3]
    split = extended.reshape(members, basis_count, out_ch, ext_rows, ext_cols)
    accum = None
    for row_off in range(5):
        for col_off in range(5):
            window = split[:, :, :, row_off : row_off + lat_rows, col_off : col_off + lon_cols]
            taps = psi[:, :, row_off, col_off][None, :, None, :, None]
            contrib = jnp.sum(taps * window, axis=1)
            accum = contrib if accum is None else accum + contrib
    return accum


def shards(nodes, norm_gain, w_qkv, w_out, w_latent, neighbours, assignment, psi, w_dec):
    members, rows, width = nodes.shape
    head_dim = width // HEADS
    count = neighbours.shape[1]
    normed = layer_norm(nodes, norm_gain)
    flat = normed.reshape(-1, width)
    reg_here = lax.axis_index("reg")
    lon_here = lax.axis_index("lon")
    sectors = lax.axis_size("lon")
    listed = neighbours[0]
    step_reg = listed // sectors - reg_here
    step_lon = (listed % sectors - lon_here + 1) % sectors - 1
    slots = (step_reg + 1) * 3 + step_lon + 1
    projected = jnp.dot(flat, w_qkv, preferred_element_type=jnp.float32)
    queries = projected[:, :width].astype(jnp.bfloat16)
    keyvals = projected[:, width:].astype(jnp.bfloat16).reshape(1, 1, members, rows, 2 * width)
    wider = with_halo(keyvals, (("reg", 0),), 1, False)
    wider = with_halo(wider, (("lon", 1),), 1, True)
    candidates = wider.reshape(9, members, rows, 2 * width)
    selected = jnp.take(candidates, slots, axis=0)
    keyset = selected.transpose(1, 0, 2, 3).reshape(members, count * rows, 2 * width)
    key_part = keyset[..., :width].reshape(members, count * rows, HEADS, head_dim)
    value_part = keyset[..., width:].reshape(members, count * rows, HEADS, head_dim)
    query_part = queries.reshape(members, rows, HEADS, head_dim)
    scale = 1.0 / head_dim**0.5
    scores = (
        jnp.einsum("mqhd,mkhd->mhqk", query_part, key_part, preferred_element_type=jnp.float32)
        * scale
    )
    top = jnp.max(scores, axis=-1, keepdims=True)
    expo = jnp.exp(scores - top)
    total = jnp.sum(expo, axis=-1, keepdims=True)
    summed = jnp.einsum(
        "mhqk,mkhd->mqhd", expo.astype(jnp.bfloat16), value_part, preferred_element_type=jnp.float32
    )
    attended = (summed / total.transpose(0, 2, 1, 3)).astype(jnp.bfloat16).reshape(-1, width)
    state = (
        nodes.reshape(-1, width).astype(jnp.float32)
        + jnp.dot(attended, w_out, preferred_element_type=jnp.float32)
    ).astype(jnp.bfloat16)
    latent = jax.nn.silu(jnp.dot(state, w_latent, preferred_element_type=jnp.float32)).astype(
        jnp.bfloat16
    )
    channels = w_latent.shape[1]
    latent = latent.reshape(members, rows, channels)
    lat_rows, lon_cols = assignment.shape
    local_nodes = (assignment % rows).reshape(-1)
    grid = jnp.take(latent, local_nodes, axis=1).reshape(members, lat_rows, lon_cols, channels)
    basis_count = psi.shape[0]
    out_ch = w_dec.shape[2]
    mixing = w_dec.transpose(1, 0, 2).reshape(channels, basis_count * out_ch)
    extended = with_halo(grid, (("reg", 1),), 2, False)
    extended = with_halo(extended, (("lon", 2),), 2, True)
    mixed = jnp.einsum("mijc,cn->mnij", extended, mixing, preferred_element_type=jnp.float32)
    accum = apply_taps(mixed, psi, lat_rows, lon_cols, basis_count, out_ch)
    fields = accum.astype(jnp.bfloat16)
    return (state.reshape(members, rows, width), fields)


def solution(mesh):
    in_specs = (
        P(None, ("reg", "lon"), None),
        P(),
        P(),
        P(),
        P(),
        P(("reg", "lon"), None),
        P("reg", "lon"),
        P(None, "reg", None, None),
        P(),
    )
    out_specs = (P(None, ("reg", "lon"), None), P(None, None, "reg", "lon"))
    return jax.shard_map(shards, mesh=mesh, in_specs=in_specs, out_specs=out_specs, check_vma=False)
```

profile of v0, /device:TPU:97, one launch (start us, length us, event | category | flops | bytes accessed | tf_op | source)
XLA Modules:
  0.0 124.4 jit_solution(10424569703981894242)
XLA Ops:
  0.7 1.1 convert_reduce_fusion
  1.8 1.1 fusion.51
  2.9 1.3 %convolution_convert_fusion = bf16[128,1536]{1,0:T(8,128)(2,1)S(1)} fusion(bf16[512,1536]{1,0:T(8,128)(2,1)S(1)} %copy-done, bf16[1,128,512]{2,1,0:T(8,128)(2,1)} %param.9, f32[512]{0:T(512)} %param.10, f32[128]{0:T(128)S(1)} %add_rsqrt_fusion, f32[128]{0:T(128)S(1)} %broadcast_multiply_fusion), kind=kOutput, calls=%fused_computation.9 | convolution fusion | flops 201850880 | bytes 2100224 | tf_op jit(solution)/shard_map/dot_general | solution.py:57
  4.3 5.3 %collective-permute-start = (bf16[1,1,1,128,1024]{4,3,2,1,0:T(8,128)(2,1)S(1)}, bf16[1,1,1,128,1024]{4,3,2,1,0:T(8,128)(2,1)S(1)}, u32[]{:S(2)}, u32[]{:S(2)}) collective-permute-start(bf16[1,1,1,128,1024]{4,3,2,1,0:T(8,128)(2,1)S(1)} %slice_bitcast_fusion), channel_id=1, source_target_pairs={{0,16},{16,32},{32,48},{48,64},{64,80},{80,96},{96,112},{112,128},... | collective-permute-start | bytes 786440 | tf_op jit(solution)/shard_map/ppermute | solution.py:16
  9.6 1.9 %collective-permute-start.1 = (bf16[1,1,1,128,1024]{4,3,2,1,0:T(8,128)(2,1)S(1)}, bf16[1,1,1,128,1024]{4,3,2,1,0:T(8,128)(2,1)S(1)}, u32[]{:S(2)}, u32[]{:S(2)}) collective-permute-start(bf16[1,1,1,128,1024]{4,3,2,1,0:T(8,128)(2,1)S(1)} %slice_bitcast_fusion), channel_id=1, source_target_pairs={{16,0},{32,16},{48,32},{64,48},{80,64},{96,80},{112,96},{128,112},... | collective-permute-start | bytes 786440 | tf_op jit(solution)/shard_map/ppermute | solution.py:17
  11.6 1.3 %collective-permute-done = bf16[1,1,1,128,1024]{4,3,2,1,0:T(8,128)(2,1)S(1)} collective-permute-done((bf16[1,1,1,128,1024]{4,3,2,1,0:T(8,128)(2,1)S(1)}, bf16[1,1,1,128,1024]{4,3,2,1,0:T(8,128)(2,1)S(1)}, u32[]{:S(2)}, u32[]{:S(2)}) %collective-permute-start) | collective-permute-done | bytes 262176 | tf_op jit(solution)/shard_map/ppermute | solution.py:16
  12.9 5.6 %collective-permute-done.1 = bf16[1,1,1,128,1024]{4,3,2,1,0:T(8,128)(2,1)S(1)} collective-permute-done((bf16[1,1,1,128,1024]{4,3,2,1,0:T(8,128)(2,1)S(1)}, bf16[1,1,1,128,1024]{4,3,2,1,0:T(8,128)(2,1)S(1)}, u32[]{:S(2)}, u32[]{:S(2)}) %collective-permute-start.1) | collective-permute-done | bytes 262176 | tf_op jit(solution)/shard_map/ppermute | solution.py:17
  19.5 3.1 %collective-permute-start.2 = (bf16[3,1,1,128,1024]{4,3,2,1,0:T(8,128)(2,1)}, bf16[3,1,1,128,1024]{4,3,2,1,0:T(8,128)(2,1)S(1)}, u32[]{:S(2)}, u32[]{:S(2)}) collective-permute-start(bf16[3,1,1,128,1024]{4,3,2,1,0:T(8,128)(2,1)} %pad_maximum_fusion.1), channel_id=1, source_target_pairs={{0,1},{1,2},{2,3},{3,4},{4,5},{5,6},{6,7},{7,8},{8,9},{9,10},{10,1... | collective-permute-start | bytes 2359304 | tf_op jit(solution)/shard_map/ppermute | solution.py:16
  22.6 5.6 %collective-permute-start.3 = (bf16[3,1,1,128,1024]{4,3,2,1,0:T(8,128)(2,1)}, bf16[3,1,1,128,1024]{4,3,2,1,0:T(8,128)(2,1)}, u32[]{:S(2)}, u32[]{:S(2)}) collective-permute-start(bf16[3,1,1,128,1024]{4,3,2,1,0:T(8,128)(2,1)} %pad_maximum_fusion.1), channel_id=1, source_target_pairs={{1,0},{2,1},{3,2},{4,3},{5,4},{6,5},{7,6},{8,7},{9,8},{10,9},{11,1... | collective-permute-start | bytes 2359304 | tf_op jit(solution)/shard_map/ppermute | solution.py:17
  28.9 1.7 %copy.17 = bf16[128,512]{0,1:T(8,128)(2,1)} copy(bf16[128,512]{1,0:T(8,128)(2,1)} %slice.232) | data formatting | bytes 262144 | tf_op jit(solution)/shard_map/slice | solution.py:58
  30.7 9.8 %collective-permute-done.2 = bf16[3,1,1,128,1024]{4,3,2,1,0:T(8,128)(2,1)S(1)} collective-permute-done((bf16[3,1,1,128,1024]{4,3,2,1,0:T(8,128)(2,1)}, bf16[3,1,1,128,1024]{4,3,2,1,0:T(8,128)(2,1)S(1)}, u32[]{:S(2)}, u32[]{:S(2)}) %collective-permute-start.2) | collective-permute-done | bytes 786464 | tf_op jit(solution)/shard_map/ppermute | solution.py:16
  40.5 1.9 %collective-permute-done.3 = bf16[3,1,1,128,1024]{4,3,2,1,0:T(8,128)(2,1)} collective-permute-done((bf16[3,1,1,128,1024]{4,3,2,1,0:T(8,128)(2,1)}, bf16[3,1,1,128,1024]{4,3,2,1,0:T(8,128)(2,1)}, u32[]{:S(2)}, u32[]{:S(2)}) %collective-permute-start.3) | collective-permute-done | bytes 786464 | tf_op jit(solution)/shard_map/ppermute | solution.py:17
  42.4 2.6 %pad_maximum_fusion = bf16[3,3,1,128,1024]{4,3,2,1,0:T(8,128)(2,1)} fusion(bf16[3,1,1,128,1024]{4,3,2,1,0:T(8,128)(2,1)} %collective-permute-done.3, bf16[1,1,1,128,1024]{4,3,2,1,0:T(8,128)(2,1)S(1)} %collective-permute-done.1, bf16[1,1,1,128,1024]{4,3,2,1,0:T(8,128)(2,1)S(1)} %slice_bitcast_fusion, ...), kind=kLoop, calls=%fused_computation.10 | loop fusion | flops 4718592 | bytes 4718592 | tf_op jit(solution)/shard_map/concatenate | solution.py:18
  44.9 2.3 %gather_fusion = bf16[5,128,1024]{2,1,0:T(8,128)(2,1)S(1)} fusion(bf16[9,128,1024]{2,1,0:T(8,128)(2,1)} %bitcast.172, s32[1024]{0:T(1024)S(1)} %pad_clamp_fusion.1), kind=kCustom, calls=%fused_computation | custom fusion | bytes 2621460 | tf_op jit(solution)/shard_map/jit(_take)/gather | solution.py:63
  47.2 1.5 %copy.16 = bf16[1,640,1024]{1,2,0:T(8,128)(2,1)} copy(bf16[1,640,1024]{2,1,0:T(8,128)(2,1)S(1)} %bitcast.173) | data formatting | bytes 2621440 | tf_op jit(solution)/shard_map/jit(_take)/gather | solution.py:63
  48.7 1.5 %broadcast_select_fusion = bf16[1,640,1024]{1,2,0:T(8,128)(2,1)S(1)} fusion(bf16[1,640,1024]{1,2,0:T(8,128)(2,1)} %copy.16, pred[640]{0:T(1024)(128)(4,1)S(1)} %broadcast_bitcast_fusion), kind=kLoop, calls=%fused_computation.71 | loop fusion | flops 655360 | bytes 2622080 | tf_op jit(solution)/shard_map/jit(_take)/select_n | solution.py:63
  52.1 1.4 %fusion = f32[16,128]{1,0:T(8,128)S(1)} fusion(f32[16,128,640]{2,1,0:T(8,128)S(1)} %get-tuple-element.61, f32[16,128]{1,0:T(8,128)S(1)} %get-tuple-element.60), kind=kLoop, calls=%fused_computation.4 | loop fusion | flops 3930112 | bytes 5259264 | tf_op jit(solution)/shard_map/reduce_sum | solution.py:75
  53.5 1.1 fusion.46
  55.9 2.0 %gather_fusion.1 = bf16[512,512]{1,0:T(8,128)(2,1)S(1)} fusion(bf16[128,512]{1,0:T(8,128)(2,1)S(1)} %multiply_convert_fusion, s32[1024]{0:T(1024)S(1)} %pad_clamp_fusion), kind=kCustom, calls=%fused_computation.1 | custom fusion | bytes 1050624 | tf_op jit(solution)/shard_map/jit(_take)/gather | solution.py:91
  58.0 6.3 %collective-permute-start.4 = (bf16[1,2,256,512]{3,2,1,0:T(8,128)(2,1)S(1)}, bf16[1,2,256,512]{3,2,1,0:T(8,128)(2,1)S(1)}, u32[]{:S(2)}, u32[]{:S(2)}) collective-permute-start(bf16[1,2,256,512]{3,2,1,0:T(8,128)(2,1)S(1)} %broadcast_select_fusion.1), channel_id=1, source_target_pairs={{0,16},{16,32},{32,48},{48,64},{64,80},{80,96},{96,112},{112,128},... | collective-permute-start | bytes 1572872 | tf_op jit(solution)/shard_map/ppermute | solution.py:16
  64.3 1.9 %collective-permute-start.5 = (bf16[1,2,256,512]{3,2,1,0:T(8,128)(2,1)S(1)}, bf16[1,2,256,512]{3,2,1,0:T(8,128)(2,1)S(1)}, u32[]{:S(2)}, u32[]{:S(2)}) collective-permute-start(bf16[1,2,256,512]{3,2,1,0:T(8,128)(2,1)S(1)} %broadcast_select_fusion.1), channel_id=1, source_target_pairs={{16,0},{32,16},{48,32},{64,48},{80,64},{96,80},{112,96},{128,112},... | collective-permute-start | bytes 1572872 | tf_op jit(solution)/shard_map/ppermute | solution.py:17
  66.8 3.6 %collective-permute-done.4 = bf16[1,2,256,512]{3,2,1,0:T(8,128)(2,1)S(1)} collective-permute-done((bf16[1,2,256,512]{3,2,1,0:T(8,128)(2,1)S(1)}, bf16[1,2,256,512]{3,2,1,0:T(8,128)(2,1)S(1)}, u32[]{:S(2)}, u32[]{:S(2)}) %collective-permute-start.4) | collective-permute-done | bytes 524320 | tf_op jit(solution)/shard_map/ppermute | solution.py:16
  70.4 5.6 %collective-permute-done.5 = bf16[1,2,256,512]{3,2,1,0:T(8,128)(2,1)S(1)} collective-permute-done((bf16[1,2,256,512]{3,2,1,0:T(8,128)(2,1)S(1)}, bf16[1,2,256,512]{3,2,1,0:T(8,128)(2,1)S(1)}, u32[]{:S(2)}, u32[]{:S(2)}) %collective-permute-start.5) | collective-permute-done | bytes 524320 | tf_op jit(solution)/shard_map/ppermute | solution.py:17
  76.8 1.9 %collective-permute-start.6 = (bf16[1,6,2,512]{3,2,1,0:T(2,128)(2,1)S(1)}, bf16[1,6,2,512]{3,2,1,0:T(2,128)(2,1)}, u32[]{:S(2)}, u32[]{:S(2)}) collective-permute-start(bf16[1,6,2,512]{3,2,1,0:T(2,128)(2,1)S(1)} %get-tuple-element.31), channel_id=1, source_target_pairs={{0,1},{1,2},{2,3},{3,4},{4,5},{5,6},{6,7},{7,8},{8,9},{9,10},{10,1... | collective-permute-start | bytes 36872 | tf_op jit(solution)/shard_map/ppermute | solution.py:16
  78.7 7.6 %collective-permute-start.7 = (bf16[1,6,2,512]{3,2,1,0:T(2,128)(2,1)S(1)}, bf16[1,6,2,512]{3,2,1,0:T(2,128)(2,1)}, u32[]{:S(2)}, u32[]{:S(2)}) collective-permute-start(bf16[1,6,2,512]{3,2,1,0:T(2,128)(2,1)S(1)} %get-tuple-element.32), channel_id=1, source_target_pairs={{1,0},{2,1},{3,2},{4,3},{5,4},{6,5},{7,6},{8,7},{9,8},{10,9},{11,1... | collective-permute-start | bytes 36872 | tf_op jit(solution)/shard_map/ppermute | solution.py:17
  87.0 1.1 reshape.701
  88.0 5.0 %convolution_bitcast_fusion = f32[756,6,260]{0,2,1:T(8,128)} fusion(bf16[512,756,1]{0,1,2:T(8,128)(2,1)} %reshape.701, bf16[1,6,2,512]{3,2,1,0:T(2,128)(2,1)} %collective-permute-done.7, bf16[1,2,256,512]{3,2,1,0:T(8,128)(2,1)} %copy-done.4, bf16[1,2,256,512]{3,2,1,0:T(8,128)(2,1)S(1)} %broadcast_select_fusion.1, ...), kind=kOutput, calls=%fused_computation.11 | convolution fusion | flops 1215651840 | bytes 7089024 | tf_op jit(solution)/shard_map/mijc,cn->mnij/dot_general | solution.py:97
  93.0 6.6 %copy.18 = f32[756,6,260]{2,0,1:T(8,128)} copy(f32[756,6,260]{0,2,1:T(8,128)} %convolution_bitcast_fusion) | data formatting | bytes 9434880 | tf_op jit(solution)/shard_map/mijc,cn->mnij/dot_general | solution.py:97
  99.6 7.4 %transpose.46 = f32[1,9,84,6,260]{4,2,1,3,0:T(8,128)} reshape(f32[756,6,260]{2,0,1:T(8,128)} %copy.18) | data formatting | bytes 9434880 | tf_op jit(solution)/shard_map/reshape;mijc,cn->mnij/transpose | solution.py:33
  107.1 9.0 %fusion.28 = (f32[84,2,256]{2,0,1:T(8,128)S(1)}, f32[84,2,256]{2,0,1:T(8,128)S(1)}, f32[84,2,256]{2,0,1:T(8,128)S(1)}, f32[84,2,256]{2,0,1:T(8,128)S(1)}, f32[84...) fusion(f32[1,9,84,6,260]{4,2,1,3,0:T(8,128)} %transpose.46, ...), kind=kLoop, calls=%fused_computation.57 | loop fusion | flops 5117952 | bytes 12042744 | tf_op jit(solution)/shard_map/reduce_sum | solution.py:39
  116.2 3.3 %fusion.30 = (f32[84,2,256]{2,0,1:T(8,128)S(1)}, f32[84,2,256]{2,0,1:T(8,128)S(1)}, f32[84,2,256]{2,0,1:T(8,128)S(1)}, f32[84,2,256]{2,0,1:T(8,128)S(1)}, f32[84...) fusion(f32[1,9,84,6,260]{4,2,1,3,0:T(8,128)S(1)} %copy-done.1, ...), kind=kLoop, calls=%fused_computation.61 | loop fusion | flops 6580224 | bytes 15483528 | tf_op jit(solution)/shard_map/reduce_sum | solution.py:39
  119.5 3.8 %fusion.29 = (f32[84,2,256]{2,0,1:T(8,128)S(1)}, f32[84,2,256]{2,0,1:T(8,128)S(1)}, f32[84,2,256]{2,0,1:T(8,128)S(1)}, f32[84,2,256]{2,0,1:T(8,128)S(1)}, f32[84...) fusion(f32[1,9,84,6,260]{4,2,1,3,0:T(8,128)S(1)} %copy-done.1, ...), kind=kLoop, calls=%fused_computation.59 | loop fusion | flops 6580224 | bytes 15483528 | tf_op jit(solution)/shard_map/reduce_sum | solution.py:39
  (65 shorter events, 8.2 us)
Async XLA Ops:
  0.6 2.3 %copy-start = (bf16[512,1536]{1,0:T(8,128)(2,1)S(1)}, bf16[512,1536]{1,0:T(8,128)(2,1)}, u32[]{:S(2)}) copy-start(bf16[512,1536]{1,0:T(8,128)(2,1)} %param.11) | copy-start | bytes 4718596
  0.6 10.9 %copy-start.18 = (s32[1,5]{1,0:T(1,128)S(1)}, s32[1,5]{1,0:T(1,128)}, u32[]{:S(2)}) copy-start(s32[1,5]{1,0:T(1,128)} %param.14) | copy-start | bytes 64
  0.7 10.9 %copy-start.17 = (s32[2,256]{1,0:T(2,128)S(1)}, s32[2,256]{1,0:T(2,128)}, u32[]{:S(2)}) copy-start(s32[2,256]{1,0:T(2,128)} %param.15) | copy-start | bytes 6148
  4.3 8.6 %collective-permute-start = (bf16[1,1,1,128,1024]{4,3,2,1,0:T(8,128)(2,1)S(1)}, bf16[1,1,1,128,1024]{4,3,2,1,0:T(8,128)(2,1)S(1)}, u32[]{:S(2)}, u32[]{:S(2)}) collective-permute-start(bf16[1,1,1,128,1024]{4,3,2,1,0:T(8,128)(2,1)S(1)} %slice_bitcast_fusion), channel_id=1, source_target_pairs={{0,16},{16,32},{32,48},{48,64},{64,80},{80,96},{96,112},{112,128},... | collective-permute-start | bytes 786440 | tf_op jit(solution)/shard_map/ppermute | solution.py:16
  9.6 8.9 %collective-permute-start.1 = (bf16[1,1,1,128,1024]{4,3,2,1,0:T(8,128)(2,1)S(1)}, bf16[1,1,1,128,1024]{4,3,2,1,0:T(8,128)(2,1)S(1)}, u32[]{:S(2)}, u32[]{:S(2)}) collective-permute-start(bf16[1,1,1,128,1024]{4,3,2,1,0:T(8,128)(2,1)S(1)} %slice_bitcast_fusion), channel_id=1, source_target_pairs={{16,0},{32,16},{48,32},{64,48},{80,64},{96,80},{112,96},{128,112},... | collective-permute-start | bytes 786440 | tf_op jit(solution)/shard_map/ppermute | solution.py:17
  19.5 21.0 %collective-permute-start.2 = (bf16[3,1,1,128,1024]{4,3,2,1,0:T(8,128)(2,1)}, bf16[3,1,1,128,1024]{4,3,2,1,0:T(8,128)(2,1)S(1)}, u32[]{:S(2)}, u32[]{:S(2)}) collective-permute-start(bf16[3,1,1,128,1024]{4,3,2,1,0:T(8,128)(2,1)} %pad_maximum_fusion.1), channel_id=1, source_target_pairs={{0,1},{1,2},{2,3},{3,4},{4,5},{5,6},{6,7},{7,8},{8,9},{9,10},{10,1... | collective-permute-start | bytes 2359304 | tf_op jit(solution)/shard_map/ppermute | solution.py:16
  22.6 19.8 %collective-permute-start.3 = (bf16[3,1,1,128,1024]{4,3,2,1,0:T(8,128)(2,1)}, bf16[3,1,1,128,1024]{4,3,2,1,0:T(8,128)(2,1)}, u32[]{:S(2)}, u32[]{:S(2)}) collective-permute-start(bf16[3,1,1,128,1024]{4,3,2,1,0:T(8,128)(2,1)} %pad_maximum_fusion.1), channel_id=1, source_target_pairs={{1,0},{2,1},{3,2},{4,3},{5,4},{6,5},{7,6},{8,7},{9,8},{10,9},{11,1... | collective-permute-start | bytes 2359304 | tf_op jit(solution)/shard_map/ppermute | solution.py:17
  50.2 0.9 copy-start.6
  53.5 1.2 copy-start.2
  53.5 1.2 copy-start.5
  53.5 2.1 %copy-start.19 = (bf16[512,512]{1,0:T(8,128)(2,1)S(1)}, bf16[512,512]{1,0:T(8,128)(2,1)}, u32[]{:S(2)}) copy-start(bf16[512,512]{1,0:T(8,128)(2,1)} %param.13) | copy-start | bytes 1572868
  54.9 0.7 copy-start.7
  55.9 10.3 %copy-start.8 = (f32[9,2,5,5]{0,1,3,2:T(2,128)S(1)}, f32[9,2,5,5]{0,1,3,2:T(2,128)}, u32[]{:S(2)}) copy-start(f32[9,2,5,5]{0,1,3,2:T(2,128)} %param.16) | copy-start | bytes 5404
  57.9 29.1 %copy-start.3 = (bf16[9,512,84]{1,2,0:T(8,128)(2,1)S(1)}, bf16[9,512,84]{1,2,0:T(8,128)(2,1)}, u32[]{:S(2)}) copy-start(bf16[9,512,84]{1,2,0:T(8,128)(2,1)} %param.17) | copy-start | bytes 2322436
  58.0 12.4 %collective-permute-start.4 = (bf16[1,2,256,512]{3,2,1,0:T(8,128)(2,1)S(1)}, bf16[1,2,256,512]{3,2,1,0:T(8,128)(2,1)S(1)}, u32[]{:S(2)}, u32[]{:S(2)}) collective-permute-start(bf16[1,2,256,512]{3,2,1,0:T(8,128)(2,1)S(1)} %broadcast_select_fusion.1), channel_id=1, source_target_pairs={{0,16},{16,32},{32,48},{48,64},{64,80},{80,96},{96,112},{112,128},... | collective-permute-start | bytes 1572872 | tf_op jit(solution)/shard_map/ppermute | solution.py:16
  64.3 11.7 %collective-permute-start.5 = (bf16[1,2,256,512]{3,2,1,0:T(8,128)(2,1)S(1)}, bf16[1,2,256,512]{3,2,1,0:T(8,128)(2,1)S(1)}, u32[]{:S(2)}, u32[]{:S(2)}) collective-permute-start(bf16[1,2,256,512]{3,2,1,0:T(8,128)(2,1)S(1)} %broadcast_select_fusion.1), channel_id=1, source_target_pairs={{16,0},{32,16},{48,32},{64,48},{80,64},{96,80},{112,96},{128,112},... | collective-permute-start | bytes 1572872 | tf_op jit(solution)/shard_map/ppermute | solution.py:17
  76.0 0.8 copy-start.4
  76.8 11.2 %collective-permute-start.6 = (bf16[1,6,2,512]{3,2,1,0:T(2,128)(2,1)S(1)}, bf16[1,6,2,512]{3,2,1,0:T(2,128)(2,1)}, u32[]{:S(2)}, u32[]{:S(2)}) collective-permute-start(bf16[1,6,2,512]{3,2,1,0:T(2,128)(2,1)S(1)} %get-tuple-element.31), channel_id=1, source_target_pairs={{0,1},{1,2},{2,3},{3,4},{4,5},{5,6},{6,7},{7,8},{8,9},{9,10},{10,1... | collective-permute-start | bytes 36872 | tf_op jit(solution)/shard_map/ppermute | solution.py:16
  78.7 9.3 %collective-permute-start.7 = (bf16[1,6,2,512]{3,2,1,0:T(2,128)(2,1)S(1)}, bf16[1,6,2,512]{3,2,1,0:T(2,128)(2,1)}, u32[]{:S(2)}, u32[]{:S(2)}) collective-permute-start(bf16[1,6,2,512]{3,2,1,0:T(2,128)(2,1)S(1)} %get-tuple-element.32), channel_id=1, source_target_pairs={{1,0},{2,1},{3,2},{4,3},{5,4},{6,5},{7,6},{8,7},{9,8},{10,9},{11,1... | collective-permute-start | bytes 36872 | tf_op jit(solution)/shard_map/ppermute | solution.py:17
  107.1 9.0 %copy-start.1 = (f32[1,9,84,6,260]{4,2,1,3,0:T(8,128)S(1)}, f32[1,9,84,6,260]{4,2,1,3,0:T(8,128)}, u32[]{:S(2)}) copy-start(f32[1,9,84,6,260]{4,2,1,3,0:T(8,128)} %transpose.46) | copy-start | bytes 14152324
  107.1 9.1 %copy-start.9 = (f32[9,2]{0,1:T(2,128)S(1)}, f32[9,2]{0,1:T(2,128)}, u32[]{:S(2)}) copy-start(f32[9,2]{0,1:T(2,128)} %get-tuple-element.46) | copy-start | bytes 220
  107.1 9.1 %copy-start.10 = (f32[9,2]{0,1:T(2,128)S(1)}, f32[9,2]{0,1:T(2,128)}, u32[]{:S(2)}) copy-start(f32[9,2]{0,1:T(2,128)} %get-tuple-element.47) | copy-start | bytes 220
  107.1 9.1 %copy-start.11 = (f32[9,2]{0,1:T(2,128)S(1)}, f32[9,2]{0,1:T(2,128)}, u32[]{:S(2)}) copy-start(f32[9,2]{0,1:T(2,128)} %get-tuple-element.48) | copy-start | bytes 220
  107.1 9.1 %copy-start.12 = (f32[9,2]{0,1:T(2,128)S(1)}, f32[9,2]{0,1:T(2,128)}, u32[]{:S(2)}) copy-start(f32[9,2]{0,1:T(2,128)} %get-tuple-element.49) | copy-start | bytes 220
  107.1 9.1 %copy-start.16 = (f32[9,2]{0,1:T(2,128)S(1)}, f32[9,2]{0,1:T(2,128)}, u32[]{:S(2)}) copy-start(f32[9,2]{0,1:T(2,128)} %get-tuple-element.57) | copy-start | bytes 220
  116.2 3.3 %copy-start.13 = (f32[9,2]{0,1:T(2,128)S(1)}, f32[9,2]{0,1:T(2,128)}, u32[]{:S(2)}) copy-start(f32[9,2]{0,1:T(2,128)} %get-tuple-element.56) | copy-start | bytes 220
  116.2 3.3 %copy-start.14 = (f32[9,2]{0,1:T(2,128)S(1)}, f32[9,2]{0,1:T(2,128)}, u32[]{:S(2)}) copy-start(f32[9,2]{0,1:T(2,128)} %get-tuple-element.58) | copy-start | bytes 220
  116.2 3.3 %copy-start.15 = (f32[9,2]{0,1:T(2,128)S(1)}, f32[9,2]{0,1:T(2,128)}, u32[]{:S(2)}) copy-start(f32[9,2]{0,1:T(2,128)} %get-tuple-element.59) | copy-start | bytes 220
where the time goes:
time: 125 us; the launch traced here: 124 us
  starting transfers between devices  33.7 us (27%)
  waiting for transfers between devices  27.8 us (22%)
  local copies, waits for them, and re-layouts  27.6 us (22%)
  other arithmetic  25.3 us (20%)
  matrix products  8.92 us (7%)
    ppermute x4, starting transfers between devices, with_halo(): after = lax.ppermute(leading, axis, down)  17.1 us
    ppermute x4, starting transfers between devices, with_halo(): before = lax.ppermute(last, axis, up)  16.6 us
    reduce_sum x3, other arithmetic, apply_taps(): contrib = jnp.sum(taps * window, axis=1)  16.1 us
    ppermute x4, waiting for transfers between devices, with_halo(): before = lax.ppermute(last, axis, up)  14.7 us
    ppermute x4, waiting for transfers between devices, with_halo(): after = lax.ppermute(leading, axis, down)  13.1 us
    transpose x1, local copies, waits for them, and re-layouts, apply_taps(): split = extended.reshape(members, basis_count, out_ch, ext_rows, ext_cols)  7.42 us
    dot_general x1, local copies, waits for them, and re-layouts, shards(): jnp.einsum('mijc,cn->mnij', extended, mixing, preferred_element_type=jnp....  6.6 us
    dot_general x1, matrix products, shards(): jnp.einsum('mijc,cn->mnij', extended, mixing, preferred_element_type=jnp....  5 us
  transfers between devices with their start and end apart: 8, of which 6 were waited for; matrix products, arithmetic and copies ran while one was open for 4% of the time, Pallas kernels for 0%

commit v1 on v0

v1 whole, which is shorter than its diff:
```python
import functools
import math

import jax
import jax.numpy as jnp
from jax import lax
from jax.experimental import pallas as pl
from jax.experimental.pallas import tpu as pltpu
from jax.sharding import PartitionSpec as P

MESH = pl.DeviceIdType.MESH
F32, BF16 = jnp.float32, jnp.bfloat16
HEADS = 16
CHUNKS = 2
BLK, D = 128, 512
COLS = 256
NBAS, OUT, OUTP = 9, 84, 96
NT = (((1,), (1,)), ((), ()))

OWN, LEFT, RIGHT, UP, DOWN, UL, UR, DL, DR = range(9)
STEPS = [(0, 0), (0, -1), (0, 1), (-1, 0), (1, 0), (-1, -1), (-1, 1), (1, -1), (1, 1)]
CODE = [(r + 1) * 3 + c + 1 for r, c in STEPS]

C_UP, C_DOWN, C_AUP, C_ADOWN, C_LUP, C_LDOWN, C_EL, C_ER, C_HUP, C_HDOWN = range(10)
C_LON = 10
C_DIAG = C_LON + 2 * CHUNKS
N_COPIES = C_DIAG + 4 * CHUNKS


def taps_of(blk, i):
    found = []
    for r in range(2):
        a = 2 * (blk - 1) + r - i
        if -2 <= a <= 2:
            found += [(r, e, (i * 5 + a + 2) * 5 + e) for e in range(5)]
    return found


def kernel(
    n_reg, n_lon,
    nodes_h, gain_h, wqkv_h, wout_h, wlat_h, nbr_h, asg_h, psi_h, wdec_h,
    state_o, fields_o,
    xs, gain, wqkv, wout, wlat, nbr, asg, psi, wdec, wtp,
    slots, qb, kb, vb, att, lat, edge, edges_in, halo, onehot_e,
    hot, splat, sel, hmask, hsel,
    load_sem, send_sem, recv_sem,
):
    reg, lon = lax.axis_index("reg"), lax.axis_index("lon")
    up = (lax.rem(reg + n_reg - 1, n_reg), lon)
    down = (lax.rem(reg + 1, n_reg), lon)
    left = (reg, lax.rem(lon + n_lon - 1, n_lon))
    right = (reg, lax.rem(lon + 1, n_lon))

    barrier = pltpu.get_barrier_semaphore()
    for where in (up, down, left, right):
        pl.semaphore_signal(barrier, inc=1, device_id=where, device_id_type=MESH)

    loads = [
        pltpu.make_async_copy(src, dst, load_sem.at[k])
        for k, (src, dst) in enumerate(
            [(nodes_h, xs), (gain_h, gain), (asg_h, asg.at[1]), (psi_h, psi), (nbr_h, nbr),
             (wqkv_h, wqkv), (wdec_h, wdec), (wout_h, wout), (wlat_h, wlat)]
        )
    ]
    for load in loads:
        load.start()

    def remote(k, src, dst, to):
        return pltpu.make_async_remote_copy(
            src_ref=src, dst_ref=dst, send_sem=send_sem.at[k], recv_sem=recv_sem.at[k],
            device_id=to, device_id_type=MESH,
        )

    loads[0].wait()
    loads[1].wait()
    values = xs[...].astype(F32)
    center = values - jnp.mean(values, axis=-1, keepdims=True)
    spread = jnp.mean(center * center, axis=-1, keepdims=True)
    slots[OWN] = (center * lax.rsqrt(spread + 1e-05) * gain[...]).astype(BF16)
    loads[2].wait()

    pl.semaphore_wait(barrier, 4)

    rows = BLK // CHUNKS
    copies = {}
    for c in range(CHUNKS):
        part = pl.ds(c * rows, rows)
        for side, (to, slot) in enumerate(((left, RIGHT), (right, LEFT))):
            k = C_LON + 2 * c + side
            copies[k] = remote(k, slots.at[OWN, part], slots.at[slot, part], to)
            copies[k].start()
    copies[C_UP] = remote(C_UP, slots.at[OWN], slots.at[DOWN], up)
    copies[C_DOWN] = remote(C_DOWN, slots.at[OWN], slots.at[UP], down)
    copies[C_AUP] = remote(C_AUP, asg.at[1], asg.at[2], up)
    copies[C_ADOWN] = remote(C_ADOWN, asg.at[1], asg.at[0], down)
    for k in (C_UP, C_DOWN, C_AUP, C_ADOWN):
        copies[k].start()

    def relay(c):
        part = pl.ds(c * rows, rows)
        for side, (slot, to_up, to_down) in enumerate(((RIGHT, DR, UR), (LEFT, DL, UL))):
            copies[C_LON + 2 * c + side].wait_recv()
            for v, (to, there) in enumerate(((up, to_up), (down, to_down))):
                k = C_DIAG + 4 * c + 2 * side + v
                copies[k] = remote(k, slots.at[slot, part], slots.at[there, part], to)
                copies[k].start()

    loads[3].wait()
    loads[4].wait()

    def spread_taps(k, _):
        i, a, e = k // 25, (k // 5) % 5, k % 5
        row = 2 * reg + i + a - 2
        inside = jnp.logical_and(row >= 0, row < 2 * n_reg)
        for b in range(NBAS):
            value = jnp.where(inside, psi[a, e, i, b], 0.0)
            splat[k * NBAS + b] = jnp.full((16, 128), value, F32).astype(BF16)
        return 0

    lax.fori_loop(0, 50, spread_taps, 0)

    lane = lax.broadcasted_iota(jnp.int32, (8, COLS), 1)
    node = lax.broadcasted_iota(jnp.int32, (BLK, COLS), 0)

    def one_hots(blk):
        for r in range(2):
            local = jnp.broadcast_to(asg[blk, r : r + 1, :] & (BLK - 1), (8, COLS))
            for e in range(5):
                s = e - 2
                moved = pltpu.roll(local, (-s) % COLS, 1) if s else local
                if s < 0:
                    moved = jnp.where(lane < -s, -1, moved)
                if s > 0:
                    moved = jnp.where(lane >= COLS - s, -1, moved)
                tall = jnp.concatenate([moved] * (BLK // 8), axis=0)
                hot[blk, r * 5 + e] = jnp.where(node == tall, 1.0, 0.0).astype(BF16)

    def selections(blk):
        for i in range(2):
            taps = taps_of(blk, i)

            def some(n, _, i=i, taps=taps):
                at = pl.multiple_of(n * 32, 32)
                hots = [hot[blk, r * 5 + e, pl.ds(at, 32), :] for r, e, _ in taps]
                for b in range(NBAS):
                    total = None
                    for h, (_, _, k) in zip(hots, taps, strict=True):
                        tap = splat[k * NBAS + b]
                        tap = jnp.concatenate([tap, tap], axis=0)
                        tap = jnp.concatenate([tap, tap], axis=1)
                        total = tap * h if total is None else total + tap * h
                    sel[blk, pl.ds(b * BLK + at, 32), pl.ds(i * COLS, COLS)] = total
                return 0

            lax.fori_loop(0, BLK // 32, some, 0)

    loads[5].wait()
    scale = math.log2(math.e) / math.sqrt(D // HEADS)
    projected = jnp.dot(slots[OWN], wqkv[...], preferred_element_type=F32)
    qb[...] = (projected[:, :D] * scale).astype(BF16)
    kb[CODE[OWN]] = projected[:, D : 2 * D].astype(BF16)
    vb[CODE[OWN]] = projected[:, 2 * D :].astype(BF16)

    def keys_values(first, count):
        x = slots[first : first + count].reshape(count * BLK, D)
        kv = jnp.dot(x, wqkv[:, D:], preferred_element_type=F32).astype(BF16)
        for n in range(count):
            kb[CODE[first + n]] = kv[n * BLK : (n + 1) * BLK, :D]
            vb[CODE[first + n]] = kv[n * BLK : (n + 1) * BLK, D:]

    one_hots(1)
    relay(0)
    selections(1)
    relay(1)
    keys_values(LEFT, 2)
    copies[C_AUP].wait_recv()
    copies[C_ADOWN].wait_recv()
    one_hots(0)
    one_hots(2)
    selections(0)
    copies[C_UP].wait_recv()
    copies[C_DOWN].wait_recv()
    keys_values(UP, 2)
    selections(2)

    loads[6].wait()
    for b in range(NBAS):
        wtp[pl.ds(b * OUTP, OUTP)] = jnp.concatenate(
            [wdec[b], jnp.zeros((OUTP - OUT, D), BF16)], axis=0
        )

    s_id = lax.broadcasted_iota(jnp.int32, (48, 128), 0)
    l_id = lax.broadcasted_iota(jnp.int32, (48, 128), 1)
    within = s_id % 16
    cell_row = jnp.where(s_id < 16, 0, jnp.where(s_id < 32, -2, 2)) + (within % 4) // 2
    cell_col = jnp.where(within < 4, COLS, -2) + within % 2
    out_col = jnp.where(l_id < 2, l_id, l_id + 128)
    usable = jnp.logical_and(within < 8, jnp.logical_or(l_id < 2, l_id >= 126))
    col_step = jnp.where(usable, cell_col - out_col, 100)
    for i in range(2):
        for a in range(5):
            for e in range(5):
                match = jnp.logical_and(cell_row - i == a - 2, col_step == e - 2)
                hmask[(i * 5 + a) * 5 + e] = jnp.where(match, 1.0, 0.0).astype(BF16)

    def halo_taps(b, _):
        for i in range(2):
            total = None
            for k in range(25):
                tap = splat[(i * 25 + k) * NBAS + b]
                tap = jnp.concatenate([tap] * 3, axis=0)
                term = tap * hmask[i * 25 + k]
                total = term if total is None else total + term
            at = pl.multiple_of(b * 128, 128)
            hsel[pl.ds(at, 48), pl.ds(i * 128, 128)] = total
            hsel[pl.ds(at + 48, 80), pl.ds(i * 128, 128)] = jnp.zeros((80, 128), BF16)
        return 0

    lax.fori_loop(0, NBAS, halo_taps, 0)
    halo[3] = jnp.zeros((16, D), BF16)

    own = asg[1] & (BLK - 1)
    lane1 = lax.broadcasted_iota(jnp.int32, (8, 128), 1)
    marks = jnp.full((8, 128), -1, jnp.int32)
    for r in range(2):
        for side in range(2):
            piece = jnp.broadcast_to(own[r : r + 1, side * 128 : side * 128 + 128], (8, 128))
            first, source = 4 * side + 2 * r, 126 * side
            moved = pltpu.roll(piece, (first - source) % 128, 1) if first != source else piece
            marks = jnp.where(jnp.logical_and(lane1 >= first, lane1 < first + 2), moved, marks)
    tall = jnp.concatenate([marks] * (BLK // 8), axis=0)
    hits = jnp.where(node[:, :128] == tall, 1.0, 0.0)
    onehot_e[...] = jnp.transpose(hits)[:16].astype(BF16)

    for c in range(CHUNKS):
        for n in range(4):
            copies[C_DIAG + 4 * c + n].wait_recv()
    keys_values(UL, 4)

    slot = []
    for n in range(5):
        there = nbr[0, n]
        row_step = there // n_lon - reg
        col_step = lax.rem(there % n_lon - lon + 1 + n_lon, n_lon) - 1
        code = (row_step + 1) * 3 + col_step + 1
        slot.append(jnp.clip(code, 0, 8))
    head_lane = lax.broadcasted_iota(jnp.int32, (BLK, 128), 1) // 32
    ones = jnp.ones((5 * BLK, 128), BF16)
    zero = jnp.zeros((BLK, 128), BF16)
    for g in range(4):
        part = pl.ds(g * 128, 128)
        keys = jnp.concatenate([kb[s, :, part] for s in slot], axis=0)
        vals = jnp.concatenate([vb[s, :, part] for s in slot], axis=0)
        q = qb[:, part]
        wide = jnp.concatenate([jnp.where(head_lane == h, q, zero) for h in range(4)], axis=0)
        scores = lax.dot_general(wide, keys, NT, preferred_element_type=F32)
        top = jnp.max(scores, axis=-1, keepdims=True)
        weights = jnp.exp2(scores - top).astype(BF16)
        summed = jnp.dot(
            weights, jnp.concatenate([vals, ones], axis=1), preferred_element_type=F32
        )
        num, den = summed[:BLK, :128], summed[:BLK, 128:]
        for h in range(1, 4):
            mine = head_lane == h
            num = jnp.where(mine, summed[h * BLK : (h + 1) * BLK, :128], num)
            den = jnp.where(mine, summed[h * BLK : (h + 1) * BLK, 128:], den)
        att[:, part] = (num / den).astype(BF16)

    loads[7].wait()
    loads[8].wait()
    state = (
        xs[...].astype(F32) + jnp.dot(att[...], wout[...], preferred_element_type=F32)
    ).astype(BF16)
    state_o[...] = state
    v = jnp.dot(state, wlat[...], preferred_element_type=F32)
    lat[1] = (v / (1.0 + jnp.exp(-v))).astype(BF16)

    copies[C_LUP] = remote(C_LUP, lat.at[1], lat.at[2], up)
    copies[C_LDOWN] = remote(C_LDOWN, lat.at[1], lat.at[0], down)
    copies[C_LUP].start()
    copies[C_LDOWN].start()
    edge[...] = jnp.dot(onehot_e[...], lat[1], preferred_element_type=F32).astype(BF16)
    copies[C_EL] = remote(C_EL, edge, edges_in.at[0], left)
    copies[C_ER] = remote(C_ER, edge, edges_in.at[1], right)
    copies[C_EL].start()
    copies[C_ER].start()

    def mixed(nodes_in):
        return lax.dot_general(wtp[...], nodes_in, NT, preferred_element_type=F32).astype(BF16)

    def decode(blk):
        z = mixed(lat[blk])
        z = jnp.concatenate([z[b * OUTP : (b + 1) * OUTP] for b in range(NBAS)], axis=1)
        return jnp.dot(z, sel[blk], preferred_element_type=F32)

    total = decode(1)

    copies[C_EL].wait_recv()
    copies[C_ER].wait_recv()
    first4 = lax.broadcasted_iota(jnp.int32, (16, D), 0) < 4
    halo[0] = jnp.where(first4, edges_in[0].astype(F32), edges_in[1].astype(F32)).astype(BF16)
    copies[C_HUP] = remote(C_HUP, halo.at[0], halo.at[2], up)
    copies[C_HDOWN] = remote(C_HDOWN, halo.at[0], halo.at[1], down)
    copies[C_HUP].start()
    copies[C_HDOWN].start()

    copies[C_LUP].wait_recv()
    total += decode(2)
    copies[C_LDOWN].wait_recv()
    total += decode(0)
    copies[C_HUP].wait_recv()
    copies[C_HDOWN].wait_recv()
    z = mixed(jnp.concatenate([halo[0], halo[1], halo[2]] + [halo[3]] * 5, axis=0))
    z = jnp.concatenate([z[b * OUTP : (b + 1) * OUTP] for b in range(NBAS)], axis=1)
    sides = jnp.dot(z, hsel[...], preferred_element_type=F32)
    lane2 = lax.broadcasted_iota(jnp.int32, (OUTP, 128), 1)
    for i in range(2):
        side = sides[:, i * 128 : (i + 1) * 128]
        at_left = jnp.where(lane2 < 2, side, 0.0)
        at_right = jnp.where(lane2 >= 126, side, 0.0)
        whole = total[:, i * COLS : (i + 1) * COLS] + jnp.concatenate([at_left, at_right], axis=1)
        fields_o[i] = whole[:OUT].astype(BF16)

    for copy in copies.values():
        copy.wait_send()


def shards(sizes, nodes, norm_gain, w_qkv, w_out, w_latent, neighbours, assignment, psi, w_dec):
    anywhere = pl.BlockSpec(memory_space=pl.ANY)
    vmem = pl.BlockSpec(memory_space=pltpu.VMEM)
    state, fields = pl.pallas_call(
        functools.partial(kernel, *sizes),
        out_shape=(
            jax.ShapeDtypeStruct((BLK, D), BF16),
            jax.ShapeDtypeStruct((2, OUT, COLS), BF16),
        ),
        in_specs=[anywhere] * 9,
        out_specs=(vmem, vmem),
        scratch_shapes=[
            pltpu.VMEM((BLK, D), BF16),
            pltpu.VMEM((1, D), F32),
            pltpu.VMEM((D, 3 * D), BF16),
            pltpu.VMEM((D, D), BF16),
            pltpu.VMEM((D, D), BF16),
            pltpu.SMEM((1, 5), jnp.int32),
            pltpu.VMEM((3, 2, COLS), jnp.int32),
            pltpu.SMEM((5, 5, 2, NBAS), F32),
            pltpu.VMEM((NBAS, OUT, D), BF16),
            pltpu.VMEM((NBAS * OUTP, D), BF16),
            pltpu.VMEM((9, BLK, D), BF16),
            pltpu.VMEM((BLK, D), BF16),
            pltpu.VMEM((9, BLK, D), BF16),
            pltpu.VMEM((9, BLK, D), BF16),
            pltpu.VMEM((BLK, D), BF16),
            pltpu.VMEM((3, BLK, D), BF16),
            pltpu.VMEM((16, D), BF16),
            pltpu.VMEM((2, 16, D), BF16),
            pltpu.VMEM((4, 16, D), BF16),
            pltpu.VMEM((16, 128), BF16),
            pltpu.VMEM((3, 10, BLK, COLS), BF16),
            pltpu.VMEM((50 * NBAS, 16, 128), BF16),
            pltpu.VMEM((3, NBAS * BLK, 2 * COLS), BF16),
            pltpu.VMEM((50, 48, 128), BF16),
            pltpu.VMEM((NBAS * 128, 256), BF16),
            pltpu.SemaphoreType.DMA((9,)),
            pltpu.SemaphoreType.DMA((N_COPIES,)),
            pltpu.SemaphoreType.DMA((N_COPIES,)),
        ],
        compiler_params=pltpu.CompilerParams(
            collective_id=0, has_side_effects=True, vmem_limit_bytes=56 * 2**20
        ),
    )(
        nodes[0], norm_gain[None], w_qkv, w_out, w_latent, neighbours, assignment,
        psi.transpose(2, 3, 1, 0), w_dec.transpose(0, 2, 1),
    )
    return state[None], fields.transpose(1, 0, 2)[None]


def solution(mesh):
    sizes = (mesh.shape["reg"], mesh.shape["lon"])
    in_specs = (
        P(None, ("reg", "lon"), None),
        P(),
        P(),
        P(),
        P(),
        P(("reg", "lon"), None),
        P("reg", "lon"),
        P(None, "reg", None, None),
        P(),
    )
    out_specs = (P(None, ("reg", "lon"), None), P(None, None, "reg", "lon"))
    return jax.shard_map(
        functools.partial(shards, sizes),
        mesh=mesh,
        in_specs=in_specs,
        out_specs=out_specs,
        check_vma=False,
    )
```

time: 125 us -> 38.9 us (0.31)
  the two profiles are of different devices: /device:TPU:97 before, /device:TPU:1 now
where the time goes in v1:
time: 38.9 us; the launch traced here: 38.7 us
  Pallas kernels  34.9 us (90%)
  local copies, waits for them, and re-layouts  3.16 us (8%)
  between operations  0.64 us (2%)
    pallas_call x1, Pallas kernels, shards(): pl.pallas_call(functools.partial(kernel, *sizes), out_shape=(jax.ShapeDty...  34.9 us
    unnamed x2, local copies, waits for them, and re-layouts  3.16 us

profile of v1, /device:TPU:1, one launch (start us, length us, event | category | flops | bytes accessed | tf_op | source)
XLA Modules:
  0.0 38.7 jit_solution(776728115072910389)
XLA Ops:
  0.6 34.9 %shard_map.104 = (bf16[128,512]{1,0:T(8,128)(2,1)}, bf16[2,84,256]{2,1,0:T(8,128)(2,1)}) custom-call(bf16[128,512]{1,0:T(8,128)(2,1)} %bitcast.9, f32[1,512]{1,0:T(1,128)} %bitcast.13, bf16[512,1536]{1,0:T(8,128)(2,1)} %wqkv_h.1, bf16[512,512]{1,0:T(8,128)(2,1)} %wout_h.1, bf16[512,512]{1,0:T(8,128)(2,1)} %wlat_h.1, s32[1,5]{1,0:T(1,128)} %nbr_h.1, ...), custom_call_target="tpu_custom_call" | custom-call | tf_op jit(solution)/shard_map/pallas_call | solution.py:331
  35.6 1.6 %copy.11 = bf16[1,84,2,256]{3,2,1,0:T(2,128)(2,1)} copy(bf16[1,84,2,256]{3,1,2,0:T(8,128)(2,1)} %bitcast.11) | data formatting | bytes 172032
  37.2 1.6 %copy.13 = bf16[1,128,512]{2,1,0:T(8,128)(2,1)} copy(bf16[1,128,512]{2,1,0:T(8,128)(2,1)} %bitcast.10) | data formatting | bytes 262144

commit v2 on v1

--- a/solution.py
+++ b/solution.py
@@ -11,38 +11,31 @@
 MESH = pl.DeviceIdType.MESH
 F32, BF16 = jnp.float32, jnp.bfloat16
 HEADS = 16
-CHUNKS = 2
+CHUNKS = 4
 BLK, D = 128, 512
 COLS = 256
 NBAS, OUT, OUTP = 9, 84, 96
 NT = (((1,), (1,)), ((), ()))
+FAR = [(0, -2), (0, -1), (1, -2), (0, 2), (1, 1), (1, 2)]
 
 OWN, LEFT, RIGHT, UP, DOWN, UL, UR, DL, DR = range(9)
 STEPS = [(0, 0), (0, -1), (0, 1), (-1, 0), (1, 0), (-1, -1), (-1, 1), (1, -1), (1, 1)]
 CODE = [(r + 1) * 3 + c + 1 for r, c in STEPS]
 
-C_UP, C_DOWN, C_AUP, C_ADOWN, C_LUP, C_LDOWN, C_EL, C_ER, C_HUP, C_HDOWN = range(10)
-C_LON = 10
+C_UP, C_DOWN, C_AUP, C_ADOWN, C_LUP, C_LDOWN = range(6)
+C_EDGE = 6
+C_LON = 12
 C_DIAG = C_LON + 2 * CHUNKS
 N_COPIES = C_DIAG + 4 * CHUNKS
-
-
-def taps_of(blk, i):
-    found = []
-    for r in range(2):
-        a = 2 * (blk - 1) + r - i
-        if -2 <= a <= 2:
-            found += [(r, e, (i * 5 + a + 2) * 5 + e) for e in range(5)]
-    return found
 
 
 def kernel(
     n_reg, n_lon,
     nodes_h, gain_h, wqkv_h, wout_h, wlat_h, nbr_h, asg_h, psi_h, wdec_h,
     state_o, fields_o,
-    xs, gain, wqkv, wout, wlat, nbr, asg, psi, wdec, wtp,
-    slots, qb, kb, vb, att, lat, edge, edges_in, halo, onehot_e,
-    hot, splat, sel, hmask, hsel,
+    xs, gain, wqkv, wout, wlat, nbr, asg, psi, psi_s, wdec, wtp,
+    slots, qb, kb, vb, att, lat, edge, edges_in, onehot_e,
+    hot, kron, hsel, splat, sel,
     load_sem, send_sem, recv_sem,
 ):
     reg, lon = lax.axis_index("reg"), lax.axis_index("lon")
@@ -50,6 +43,7 @@
     down = (lax.rem(reg + 1, n_reg), lon)
     left = (reg, lax.rem(lon + n_lon - 1, n_lon))
     right = (reg, lax.rem(lon + 1, n_lon))
+    corners = [(v[0], h[1]) for v in (up, down) for h in (left, right)]
 
     barrier = pltpu.get_barrier_semaphore()
     for where in (up, down, left, right):
@@ -59,7 +53,7 @@
         pltpu.make_async_copy(src, dst, load_sem.at[k])
         for k, (src, dst) in enumerate(
             [(nodes_h, xs), (gain_h, gain), (asg_h, asg.at[1]), (psi_h, psi), (nbr_h, nbr),
-             (wqkv_h, wqkv), (wdec_h, wdec), (wout_h, wout), (wlat_h, wlat)]
+             (wqkv_h, wqkv), (wdec_h, wdec), (wout_h, wout), (wlat_h, wlat), (psi_h, psi_s)]
         )
     ]
     for load in loads:
@@ -105,20 +99,6 @@
                 copies[k] = remote(k, slots.at[slot, part], slots.at[there, part], to)
                 copies[k].start()
 
-    loads[3].wait()
-    loads[4].wait()
-
-    def spread_taps(k, _):
-        i, a, e = k // 25, (k // 5) % 5, k % 5
-        row = 2 * reg + i + a - 2
-        inside = jnp.logical_and(row >= 0, row < 2 * n_reg)
-        for b in range(NBAS):
-            value = jnp.where(inside, psi[a, e, i, b], 0.0)
-            splat[k * NBAS + b] = jnp.full((16, 128), value, F32).astype(BF16)
-        return 0
-
-    lax.fori_loop(0, 50, spread_taps, 0)
-
     lane = lax.broadcasted_iota(jnp.int32, (8, COLS), 1)
     node = lax.broadcasted_iota(jnp.int32, (BLK, COLS), 0)
 
@@ -133,26 +113,104 @@
                 if s > 0:
                     moved = jnp.where(lane >= COLS - s, -1, moved)
                 tall = jnp.concatenate([moved] * (BLK // 8), axis=0)
-                hot[blk, r * 5 + e] = jnp.where(node == tall, 1.0, 0.0).astype(BF16)
+                at = (r * 5 + e) * BLK
+                hot[blk, at : at + BLK] = jnp.where(node == tall, 1.0, 0.0).astype(BF16)
+
+    def iota(shape, dim):
+        return lax.broadcasted_iota(jnp.int32, shape, dim)
+
+    def ones_where(condition):
+        return jnp.where(condition, 1.0, 0.0).astype(BF16)
+
+    def inside(row):
+        row = row + 2 * reg
+        return jnp.logical_and(row >= 0, row < 2 * n_reg)
+
+    def taps():
+        return psi[...].reshape(50, NBAS).astype(BF16)
+
+    def tap_matrices():
+        spread = ones_where(iota((NBAS, NBAS * 16), 0) == iota((NBAS, NBAS * 16), 1) // 16)
+        wide = jnp.dot(taps(), spread, preferred_element_type=F32).astype(BF16)
+        line, tap = iota((320, 50), 0) // 16, iota((320, 50), 1)
+        i, r, e = line // 10, (line // 5) % 2, line % 5
+        diagonal = iota((320, NBAS * 16), 0) % 16 == iota((320, NBAS * 16), 1) % 16
+        pick = ones_where(tap == ((r - i + 2) * 5 + e) * 2 + i)
+        full = jnp.dot(pick, wide, preferred_element_type=F32)
+        kron[...] = jnp.where(diagonal, full, 0.0).astype(BF16)
+
+    def spread_taps():
+        for n, (i, a) in enumerate(FAR):
+
+            def at_step(e, _, n=n, i=i, a=a):
+                for b in range(NBAS):
+                    tap = jnp.where(inside(i + a), psi_s[a + 2, e, i, b], 0.0)
+                    splat[(n * 5 + e) * NBAS + b] = jnp.full((16, 128), tap, F32).astype(BF16)
+                return 0
+
+            lax.fori_loop(0, 5, at_step, 0)
 
     def selections(blk):
         for i in range(2):
-            taps = taps_of(blk, i)
-
-            def some(n, _, i=i, taps=taps):
+            taps_here = [
+                (r, e, FAR.index((i, a)) * 5 + e)
+                for r, a in ((r, 2 * (blk - 1) + r - i) for r in range(2))
+                if (i, a) in FAR
+                for e in range(5)
+            ]
+
+            def some(n, _, i=i, taps_here=taps_here):
                 at = pl.multiple_of(n * 32, 32)
-                hots = [hot[blk, r * 5 + e, pl.ds(at, 32), :] for r, e, _ in taps]
+                hots = [hot[blk, pl.ds((r * 5 + e) * BLK + at, 32), :] for r, e, _ in taps_here]
                 for b in range(NBAS):
                     total = None
-                    for h, (_, _, k) in zip(hots, taps, strict=True):
+                    for h, (_, _, k) in zip(hots, taps_here, strict=True):
                         tap = splat[k * NBAS + b]
                         tap = jnp.concatenate([tap, tap], axis=0)
                         tap = jnp.concatenate([tap, tap], axis=1)
                         total = tap * h if total is None else total + tap * h
-                    sel[blk, pl.ds(b * BLK + at, 32), pl.ds(i * COLS, COLS)] = total
+                    sel[blk // 2, pl.ds(b * BLK + at, 32), pl.ds(i * COLS, COLS)] = total
                 return 0
 
             lax.fori_loop(0, BLK // 32, some, 0)
+
+    def halo_matrix():
+        spread = ones_where(iota((NBAS * 16, NBAS), 0) // 16 == iota((NBAS * 16, NBAS), 1))
+        tall = lax.dot_general(spread, taps(), NT, preferred_element_type=F32).astype(BF16)
+        tap, column = iota((50, 1024), 0), iota((50, 1024), 1)
+        i_t, a, e = tap % 2, tap // 10 - 2, (tap // 2) % 5 - 2
+        to, cell = column // 128, column % 128
+        i_out, out_col = to // 4, jnp.where(to % 4 < 2, to % 4, to % 4 + COLS - 4)
+        within = cell % 16
+        cell_row = jnp.where(cell < 16, 0, jnp.where(cell < 32, -2, 2)) + (within % 4) // 2
+        cell_col = jnp.where(within < 4, COLS, -2) + within % 2
+        real = jnp.logical_and(cell < 48, within < 8)
+        match = jnp.logical_and(i_t == i_out, cell_row - i_out == a)
+        match = jnp.logical_and(match, cell_col - out_col == e)
+        match = jnp.logical_and(jnp.logical_and(match, real), inside(cell_row))
+        every = jnp.dot(tall, ones_where(match), preferred_element_type=F32)
+        line = iota((NBAS * 16, 128), 0) % 16
+        mine = jnp.zeros((NBAS * 16, 128), F32)
+        for to in range(8):
+            mine = jnp.where(line == to, every[:, to * 128 : (to + 1) * 128], mine)
+        for b in range(NBAS):
+            hsel[:, b * 128 : (b + 1) * 128] = mine[b * 16 : (b + 1) * 16].astype(BF16)
+
+    def keys_values(first, count):
+        x = slots[first : first + count].reshape(count * BLK, D)
+        kv = jnp.dot(x, wqkv[:, D:], preferred_element_type=F32).astype(BF16)
+        for n in range(count):
+            kb[CODE[first + n]] = kv[n * BLK : (n + 1) * BLK, :D]
+            vb[CODE[first + n]] = kv[n * BLK : (n + 1) * BLK, D:]
+
+    loads[3].wait()
+    loads[4].wait()
+    loads[9].wait()
+    one_hots(1)
+    tap_matrices()
+    halo_matrix()
+    spread_taps()
+    relay(0)
 
     loads[5].wait()
     scale = math.log2(math.e) / math.sqrt(D // HEADS)
@@ -161,63 +219,28 @@
     kb[CODE[OWN]] = projected[:, D : 2 * D].astype(BF16)
     vb[CODE[OWN]] = projected[:, 2 * D :].astype(BF16)
 
-    def keys_values(first, count):
-        x = slots[first : first + count].reshape(count * BLK, D)
-        kv = jnp.dot(x, wqkv[:, D:], preferred_element_type=F32).astype(BF16)
-        for n in range(count):
-            kb[CODE[first + n]] = kv[n * BLK : (n + 1) * BLK, :D]
-            vb[CODE[first + n]] = kv[n * BLK : (n + 1) * BLK, D:]
-
-    one_hots(1)
-    relay(0)
-    selections(1)
     relay(1)
-    keys_values(LEFT, 2)
     copies[C_AUP].wait_recv()
     copies[C_ADOWN].wait_recv()
     one_hots(0)
     one_hots(2)
+    relay(2)
     selections(0)
+    relay(3)
+    keys_values(LEFT, 2)
     copies[C_UP].wait_recv()
     copies[C_DOWN].wait_recv()
     keys_values(UP, 2)
     selections(2)
 
     loads[6].wait()
-    for b in range(NBAS):
-        wtp[pl.ds(b * OUTP, OUTP)] = jnp.concatenate(
-            [wdec[b], jnp.zeros((OUTP - OUT, D), BF16)], axis=0
-        )
-
-    s_id = lax.broadcasted_iota(jnp.int32, (48, 128), 0)
-    l_id = lax.broadcasted_iota(jnp.int32, (48, 128), 1)
-    within = s_id % 16
-    cell_row = jnp.where(s_id < 16, 0, jnp.where(s_id < 32, -2, 2)) + (within % 4) // 2
-    cell_col = jnp.where(within < 4, COLS, -2) + within % 2
-    out_col = jnp.where(l_id < 2, l_id, l_id + 128)
-    usable = jnp.logical_and(within < 8, jnp.logical_or(l_id < 2, l_id >= 126))
-    col_step = jnp.where(usable, cell_col - out_col, 100)
-    for i in range(2):
-        for a in range(5):
-            for e in range(5):
-                match = jnp.logical_and(cell_row - i == a - 2, col_step == e - 2)
-                hmask[(i * 5 + a) * 5 + e] = jnp.where(match, 1.0, 0.0).astype(BF16)
-
-    def halo_taps(b, _):
-        for i in range(2):
-            total = None
-            for k in range(25):
-                tap = splat[(i * 25 + k) * NBAS + b]
-                tap = jnp.concatenate([tap] * 3, axis=0)
-                term = tap * hmask[i * 25 + k]
-                total = term if total is None else total + term
-            at = pl.multiple_of(b * 128, 128)
-            hsel[pl.ds(at, 48), pl.ds(i * 128, 128)] = total
-            hsel[pl.ds(at + 48, 80), pl.ds(i * 128, 128)] = jnp.zeros((80, 128), BF16)
-        return 0
-
-    lax.fori_loop(0, NBAS, halo_taps, 0)
-    halo[3] = jnp.zeros((16, D), BF16)
+    for o in range(OUTP // 16):
+        for b in range(NBAS):
+            piece = wdec[b, o * 16 : min(o * 16 + 16, OUT)]
+            if piece.shape[0] < 16:
+                piece = jnp.concatenate([piece, jnp.zeros((16 - piece.shape[0], D), BF16)], axis=0)
+            at = (o * NBAS + b) * 16
+            wtp[at : at + 16] = piece
 
     own = asg[1] & (BLK - 1)
     lane1 = lax.broadcasted_iota(jnp.int32, (8, 128), 1)
@@ -280,45 +303,63 @@
     copies[C_LUP].start()
     copies[C_LDOWN].start()
     edge[...] = jnp.dot(onehot_e[...], lat[1], preferred_element_type=F32).astype(BF16)
-    copies[C_EL] = remote(C_EL, edge, edges_in.at[0], left)
-    copies[C_ER] = remote(C_ER, edge, edges_in.at[1], right)
-    copies[C_EL].start()
-    copies[C_ER].start()
+    for n, (to, there) in enumerate(zip([left, right, *corners], (0, 1, 4, 5, 2, 3), strict=True)):
+        copies[C_EDGE + n] = remote(C_EDGE + n, edge, edges_in.at[there], to)
+        copies[C_EDGE + n].start()
 
     def mixed(nodes_in):
         return lax.dot_general(wtp[...], nodes_in, NT, preferred_element_type=F32).astype(BF16)
 
-    def decode(blk):
-        z = mixed(lat[blk])
-        z = jnp.concatenate([z[b * OUTP : (b + 1) * OUTP] for b in range(NBAS)], axis=1)
-        return jnp.dot(z, sel[blk], preferred_element_type=F32)
-
-    total = decode(1)
-
-    copies[C_EL].wait_recv()
-    copies[C_ER].wait_recv()
-    first4 = lax.broadcasted_iota(jnp.int32, (16, D), 0) < 4
-    halo[0] = jnp.where(first4, edges_in[0].astype(F32), edges_in[1].astype(F32)).astype(BF16)
-    copies[C_HUP] = remote(C_HUP, halo.at[0], halo.at[2], up)
-    copies[C_HDOWN] = remote(C_HDOWN, halo.at[0], halo.at[1], down)
-    copies[C_HUP].start()
-    copies[C_HDOWN].start()
-
-    copies[C_LUP].wait_recv()
-    total += decode(2)
-    copies[C_LDOWN].wait_recv()
-    total += decode(0)
-    copies[C_HUP].wait_recv()
-    copies[C_HDOWN].wait_recv()
-    z = mixed(jnp.concatenate([halo[0], halo[1], halo[2]] + [halo[3]] * 5, axis=0))
-    z = jnp.concatenate([z[b * OUTP : (b + 1) * OUTP] for b in range(NBAS)], axis=1)
-    sides = jnp.dot(z, hsel[...], preferred_element_type=F32)
-    lane2 = lax.broadcasted_iota(jnp.int32, (OUTP, 128), 1)
+    n_out = OUTP // 16
+    high = NBAS * 16
+
+    def decode_own():
+        z = mixed(lat[1])
+        z = jnp.concatenate([z[o * high : (o + 1) * high] for o in range(n_out)], axis=1)
+        w = jnp.dot(kron[...], z, preferred_element_type=F32).astype(BF16)
+        pieces = []
+        for i in range(2):
+            for o in range(n_out):
+                line = [w[(i * 10 + k) * 16 : (i * 10 + k + 1) * 16, o * 128 : (o + 1) * 128] for k in range(10)]
+                pieces.append(jnp.concatenate(line, axis=1))
+        return jnp.dot(jnp.concatenate(pieces, axis=0), hot[1], preferred_element_type=F32)
+
+    def by_output(z):
+        lines = [
+            jnp.concatenate([z[o * high + b * 16 : o * high + b * 16 + 16] for b in range(NBAS)], axis=1)
+            for o in range(n_out)
+        ]
+        return jnp.concatenate(lines, axis=0)
+
+    def decode_far(z, k):
+        return jnp.dot(by_output(z), sel[k], preferred_element_type=F32)
+
+    total = decode_own()
+
+    even = lax.rem(reg, 2) == 0
+    near, far = jnp.where(even, 1, 0), jnp.where(even, 0, 1)
+    remote(C_LUP + 1 - near, lat.at[1], lat.at[near * 2], up).wait_recv()
+    other = decode_far(mixed(lat[near * 2]), near)
+    remote(C_LUP + 1 - far, lat.at[1], lat.at[far * 2], up).wait_recv()
+    for n in range(6):
+        copies[C_EDGE + n].wait_recv()
+    first4 = iota((16, D), 0) < 4
+    cells = []
+    for n in range(3):
+        a, b = edges_in[2 * n], edges_in[2 * n + 1]
+        cells.append(jnp.where(first4, a, b))
+    z = mixed(jnp.concatenate([lat[far * 2]] + cells + [jnp.zeros((80, D), BF16)], axis=0))
+    other += decode_far(z[:, :BLK], far)
+    z = by_output(z[:, BLK:])
+    sides = lax.dot_general(z, hsel[...], NT, preferred_element_type=F32)
+    sides = jnp.concatenate([sides, jnp.zeros((OUTP, 112), F32)], axis=1)
+    lane2 = iota((OUTP, 128), 1)
     for i in range(2):
-        side = sides[:, i * 128 : (i + 1) * 128]
-        at_left = jnp.where(lane2 < 2, side, 0.0)
-        at_right = jnp.where(lane2 >= 126, side, 0.0)
-        whole = total[:, i * COLS : (i + 1) * COLS] + jnp.concatenate([at_left, at_right], axis=1)
+        at_left = pltpu.roll(sides, (-4 * i) % 128, 1) if i else sides
+        at_left = jnp.where(lane2 < 2, at_left, 0.0)
+        at_right = jnp.where(lane2 >= 126, pltpu.roll(sides, 124 - 4 * i, 1), 0.0)
+        whole = total[i * OUTP : (i + 1) * OUTP] + other[:, i * COLS : (i + 1) * COLS]
+        whole += jnp.concatenate([at_left, at_right], axis=1)
         fields_o[i] = whole[:OUT].astype(BF16)
 
     for copy in copies.values():
@@ -331,8 +372,8 @@
     state, fields = pl.pallas_call(
         functools.partial(kernel, *sizes),
         out_shape=(
-            jax.ShapeDtypeStruct((BLK, D), BF16),
-            jax.ShapeDtypeStruct((2, OUT, COLS), BF16),
+            pltpu.VMEM((BLK, D), BF16),
+            pltpu.VMEM((2, OUT, COLS), BF16),
         ),
         in_specs=[anywhere] * 9,
         out_specs=(vmem, vmem),
@@ -344,6 +385,7 @@
             pltpu.VMEM((D, D), BF16),
             pltpu.SMEM((1, 5), jnp.int32),
             pltpu.VMEM((3, 2, COLS), jnp.int32),
+            pltpu.VMEM((5, 5, 2, NBAS), F32),
             pltpu.SMEM((5, 5, 2, NBAS), F32),
             pltpu.VMEM((NBAS, OUT, D), BF16),
             pltpu.VMEM((NBAS * OUTP, D), BF16),
@@ -354,15 +396,14 @@
             pltpu.VMEM((BLK, D), BF16),
             pltpu.VMEM((3, BLK, D), BF16),
             pltpu.VMEM((16, D), BF16),
-            pltpu.VMEM((2, 16, D), BF16),
-            pltpu.VMEM((4, 16, D), BF16),
+            pltpu.VMEM((6, 16, D), BF16),
             pltpu.VMEM((16, 128), BF16),
-            pltpu.VMEM((3, 10, BLK, COLS), BF16),
-            pltpu.VMEM((50 * NBAS, 16, 128), BF16),
-            pltpu.VMEM((3, NBAS * BLK, 2 * COLS), BF16),
-            pltpu.VMEM((50, 48, 128), BF16),
-            pltpu.VMEM((NBAS * 128, 256), BF16),
-            pltpu.SemaphoreType.DMA((9,)),
+            pltpu.VMEM((3, 10 * BLK, COLS), BF16),
+            pltpu.VMEM((320, NBAS * 16), BF16),
+            pltpu.VMEM((16, NBAS * 128), BF16),
+            pltpu.VMEM((30 * NBAS, 16, 128), BF16),
+            pltpu.VMEM((2, NBAS * BLK, 2 * COLS), BF16),
+            pltpu.SemaphoreType.DMA((10,)),
             pltpu.SemaphoreType.DMA((N_COPIES,)),
             pltpu.SemaphoreType.DMA((N_COPIES,)),
         ],

time: 38.9 us -> 35.8 us (0.920)
  local copies, waits for them, and re-layouts: 3.16 us -> 1.36 us
  Pallas kernels: 34.9 us -> 33.7 us
    unnamed x2, local copies, waits for them, and re-layouts: 3.16 us -> 1.36 us
    pallas_call x1, Pallas kernels: 34.9 us -> 33.7 us  [shards(): pl.pallas_call(functools.partial(kernel, *sizes), out_shape=(pltpu.VMEM((...]
where the time goes in v2:
time: 35.8 us; the launch traced here: 35.7 us
  Pallas kernels  33.7 us (94%)
  local copies, waits for them, and re-layouts  1.36 us (4%)
  between operations  0.64 us (2%)
    pallas_call x1, Pallas kernels, shards(): pl.pallas_call(functools.partial(kernel, *sizes), out_shape=(pltpu.VMEM((...  33.7 us
    unnamed x2, local copies, waits for them, and re-layouts  1.36 us

profile of v2, /device:TPU:1, one launch (start us, length us, event | category | flops | bytes accessed | tf_op | source)
XLA Modules:
  0.0 35.7 jit_solution(846697039456593041)
XLA Ops:
  0.6 33.7 %shard_map.104 = (bf16[128,512]{1,0:T(8,128)(2,1)S(1)}, bf16[2,84,256]{2,1,0:T(8,128)(2,1)S(1)}) custom-call(bf16[128,512]{1,0:T(8,128)(2,1)} %bitcast.11, f32[1,512]{1,0:T(1,128)} %bitcast.13, bf16[512,1536]{1,0:T(8,128)(2,1)} %wqkv_h.1, bf16[512,512]{1,0:T(8,128)(2,1)} %wout_h.1, bf16[512,512]{1,0:T(8,128)(2,1)} %wlat_h.1, s32[1,5]{1,0:T(1,128)} %nbr_h.1, ...), custom_call_target="tpu_custom_call" | custom-call | tf_op jit(solution)/shard_map/pallas_call | solution.py:372
  34.3 0.7 %copy.13 = bf16[1,128,512]{2,1,0:T(8,128)(2,1)} copy(bf16[1,128,512]{2,1,0:T(8,128)(2,1)S(1)} %bitcast.8) | data formatting | bytes 262144
  35.0 0.7 %copy.11 = bf16[1,84,2,256]{3,2,1,0:T(2,128)(2,1)} copy(bf16[1,84,2,256]{3,1,2,0:T(8,128)(2,1)S(1)} %bitcast.9) | data formatting | bytes 172032

commit v3 on v2

--- a/solution.py
+++ b/solution.py
@@ -45,9 +45,17 @@
     right = (reg, lax.rem(lon + 1, n_lon))
     corners = [(v[0], h[1]) for v in (up, down) for h in (left, right)]
 
+    has_up, has_down = reg > 0, reg < n_reg - 1
+
     barrier = pltpu.get_barrier_semaphore()
-    for where in (up, down, left, right):
+
+    def greet(where):
         pl.semaphore_signal(barrier, inc=1, device_id=where, device_id_type=MESH)
+
+    greet(left)
+    greet(right)
+    pl.when(has_up)(lambda: greet(up))
+    pl.when(has_down)(lambda: greet(down))
 
     loads = [
         pltpu.make_async_copy(src, dst, load_sem.at[k])
@@ -73,7 +81,7 @@
     slots[OWN] = (center * lax.rsqrt(spread + 1e-05) * gain[...]).astype(BF16)
     loads[2].wait()
 
-    pl.semaphore_wait(barrier, 4)
+    pl.semaphore_wait(barrier, 2 + has_up.astype(jnp.int32) + has_down.astype(jnp.int32))
 
     rows = BLK // CHUNKS
     copies = {}
@@ -87,8 +95,30 @@
     copies[C_DOWN] = remote(C_DOWN, slots.at[OWN], slots.at[UP], down)
     copies[C_AUP] = remote(C_AUP, asg.at[1], asg.at[2], up)
     copies[C_ADOWN] = remote(C_ADOWN, asg.at[1], asg.at[0], down)
-    for k in (C_UP, C_DOWN, C_AUP, C_ADOWN):
-        copies[k].start()
+
+    upward, downward = [C_UP, C_AUP], [C_DOWN, C_ADOWN]
+
+    def start_all(keys):
+        for k in keys:
+            copies[k].start()
+
+    def wait_all(keys):
+        for k in keys:
+            copies[k].wait_recv()
+
+    pl.when(has_up)(lambda: start_all([C_UP, C_AUP]))
+    pl.when(has_down)(lambda: start_all([C_DOWN, C_ADOWN]))
+
+    def clear(blk):
+        lat[blk] = jnp.zeros((BLK, D), BF16)
+        asg[blk] = jnp.zeros((2, COLS), jnp.int32)
+        for n in (0, 1):
+            edges_in[blk + 2 + n] = jnp.zeros((16, D), BF16)
+        for slot in (UP, UL, UR) if blk == 0 else (DOWN, DL, DR):
+            slots[slot] = jnp.zeros((BLK, D), BF16)
+
+    pl.when(jnp.logical_not(has_up))(lambda: clear(0))
+    pl.when(jnp.logical_not(has_down))(lambda: clear(2))
 
     def relay(c):
         part = pl.ds(c * rows, rows)
@@ -97,7 +127,11 @@
             for v, (to, there) in enumerate(((up, to_up), (down, to_down))):
                 k = C_DIAG + 4 * c + 2 * side + v
                 copies[k] = remote(k, slots.at[slot, part], slots.at[there, part], to)
-                copies[k].start()
+        ups, downs = ([C_DIAG + 4 * c + 2 * side + v for side in (0, 1)] for v in (0, 1))
+        upward.extend(ups)
+        downward.extend(downs)
+        pl.when(has_up)(lambda: start_all(ups))
+        pl.when(has_down)(lambda: start_all(downs))
 
     lane = lax.broadcasted_iota(jnp.int32, (8, COLS), 1)
     node = lax.broadcasted_iota(jnp.int32, (BLK, COLS), 0)
@@ -196,12 +230,13 @@
         for b in range(NBAS):
             hsel[:, b * 128 : (b + 1) * 128] = mine[b * 16 : (b + 1) * 16].astype(BF16)
 
-    def keys_values(first, count):
-        x = slots[first : first + count].reshape(count * BLK, D)
+    def keys_values(first, count, start=0, height=BLK):
+        part = pl.ds(start, height)
+        x = jnp.concatenate([slots[first + n, part] for n in range(count)], axis=0)
         kv = jnp.dot(x, wqkv[:, D:], preferred_element_type=F32).astype(BF16)
         for n in range(count):
-            kb[CODE[first + n]] = kv[n * BLK : (n + 1) * BLK, :D]
-            vb[CODE[first + n]] = kv[n * BLK : (n + 1) * BLK, D:]
+            kb[CODE[first + n], part] = kv[n * height : (n + 1) * height, :D]
+            vb[CODE[first + n], part] = kv[n * height : (n + 1) * height, D:]
 
     loads[3].wait()
     loads[4].wait()
@@ -220,16 +255,16 @@
     vb[CODE[OWN]] = projected[:, 2 * D :].astype(BF16)
 
     relay(1)
-    copies[C_AUP].wait_recv()
-    copies[C_ADOWN].wait_recv()
+    pl.when(has_down)(lambda: wait_all([C_AUP]))
+    pl.when(has_up)(lambda: wait_all([C_ADOWN]))
     one_hots(0)
     one_hots(2)
     relay(2)
     selections(0)
     relay(3)
     keys_values(LEFT, 2)
-    copies[C_UP].wait_recv()
-    copies[C_DOWN].wait_recv()
+    pl.when(has_down)(lambda: wait_all([C_UP]))
+    pl.when(has_up)(lambda: wait_all([C_DOWN]))
     keys_values(UP, 2)
     selections(2)
 
@@ -255,10 +290,14 @@
     hits = jnp.where(node[:, :128] == tall, 1.0, 0.0)
     onehot_e[...] = jnp.transpose(hits)[:16].astype(BF16)
 
-    for c in range(CHUNKS):
-        for n in range(4):
-            copies[C_DIAG + 4 * c + n].wait_recv()
-    keys_values(UL, 4)
+    for half in range(2):
+        chunks = range(half * CHUNKS // 2, (half + 1) * CHUNKS // 2)
+        from_down, from_up = (
+            [C_DIAG + 4 * c + 2 * side + v for c in chunks for side in (0, 1)] for v in (0, 1)
+        )
+        pl.when(has_down)(lambda keys=from_down: wait_all(keys))
+        pl.when(has_up)(lambda keys=from_up: wait_all(keys))
+        keys_values(UL, 4, half * (BLK // 2), BLK // 2)
 
     slot = []
     for n in range(5):
@@ -298,14 +337,16 @@
     v = jnp.dot(state, wlat[...], preferred_element_type=F32)
     lat[1] = (v / (1.0 + jnp.exp(-v))).astype(BF16)
 
-    copies[C_LUP] = remote(C_LUP, lat.at[1], lat.at[2], up)
-    copies[C_LDOWN] = remote(C_LDOWN, lat.at[1], lat.at[0], down)
-    copies[C_LUP].start()
-    copies[C_LDOWN].start()
     edge[...] = jnp.dot(onehot_e[...], lat[1], preferred_element_type=F32).astype(BF16)
     for n, (to, there) in enumerate(zip([left, right, *corners], (0, 1, 4, 5, 2, 3), strict=True)):
         copies[C_EDGE + n] = remote(C_EDGE + n, edge, edges_in.at[there], to)
-        copies[C_EDGE + n].start()
+    copies[C_LUP] = remote(C_LUP, lat.at[1], lat.at[2], up)
+    copies[C_LDOWN] = remote(C_LDOWN, lat.at[1], lat.at[0], down)
+    start_all([C_EDGE, C_EDGE + 1])
+    pl.when(has_up)(lambda: start_all([C_EDGE + 2, C_EDGE + 3, C_LUP]))
+    pl.when(has_down)(lambda: start_all([C_EDGE + 4, C_EDGE + 5, C_LDOWN]))
+    upward.extend([C_EDGE + 2, C_EDGE + 3, C_LUP])
+    downward.extend([C_EDGE + 4, C_EDGE + 5, C_LDOWN])
 
     def mixed(nodes_in):
         return lax.dot_general(wtp[...], nodes_in, NT, preferred_element_type=F32).astype(BF16)
@@ -340,9 +381,15 @@
     near, far = jnp.where(even, 1, 0), jnp.where(even, 0, 1)
     remote(C_LUP + 1 - near, lat.at[1], lat.at[near * 2], up).wait_recv()
     other = decode_far(mixed(lat[near * 2]), near)
-    remote(C_LUP + 1 - far, lat.at[1], lat.at[far * 2], up).wait_recv()
-    for n in range(6):
-        copies[C_EDGE + n].wait_recv()
+    has_far = jnp.logical_or(jnp.logical_and(even, has_up), jnp.logical_and(reg % 2 == 1, has_down))
+
+    @pl.when(has_far)
+    def _():
+        remote(C_LUP + 1 - far, lat.at[1], lat.at[far * 2], up).wait_recv()
+
+    wait_all([C_EDGE, C_EDGE + 1])
+    pl.when(has_down)(lambda: wait_all([C_EDGE + 2, C_EDGE + 3]))
+    pl.when(has_up)(lambda: wait_all([C_EDGE + 4, C_EDGE + 5]))
     first4 = iota((16, D), 0) < 4
     cells = []
     for n in range(3):
@@ -360,10 +407,26 @@
         at_right = jnp.where(lane2 >= 126, pltpu.roll(sides, 124 - 4 * i, 1), 0.0)
         whole = total[i * OUTP : (i + 1) * OUTP] + other[:, i * COLS : (i + 1) * COLS]
         whole += jnp.concatenate([at_left, at_right], axis=1)
-        fields_o[i] = whole[:OUT].astype(BF16)
-
-    for copy in copies.values():
-        copy.wait_send()
+        fields_o[:, i, :] = whole[:OUT].astype(BF16)
+
+    def sent(keys):
+        for k in keys:
+            copies[k].wait_send()
+
+    sent([k for k in copies if k not in upward and k not in downward])
+    pl.when(has_up)(lambda: sent(upward))
+    pl.when(has_down)(lambda: sent(downward))
+
+
+def store(state, fields, state_o, fields_o, sem):
+    copies = [
+        pltpu.make_async_copy(state, state_o, sem.at[0]),
+        pltpu.make_async_copy(fields, fields_o, sem.at[1]),
+    ]
+    for copy in copies:
+        copy.start()
+    for copy in copies:
+        copy.wait()
 
 
 def shards(sizes, nodes, norm_gain, w_qkv, w_out, w_latent, neighbours, assignment, psi, w_dec):
@@ -373,7 +436,7 @@
         functools.partial(kernel, *sizes),
         out_shape=(
             pltpu.VMEM((BLK, D), BF16),
-            pltpu.VMEM((2, OUT, COLS), BF16),
+            pltpu.VMEM((OUT, 2, COLS), BF16),
         ),
         in_specs=[anywhere] * 9,
         out_specs=(vmem, vmem),
@@ -414,7 +477,20 @@
         nodes[0], norm_gain[None], w_qkv, w_out, w_latent, neighbours, assignment,
         psi.transpose(2, 3, 1, 0), w_dec.transpose(0, 2, 1),
     )
-    return state[None], fields.transpose(1, 0, 2)[None]
+    state, fields = pl.pallas_call(
+        store,
+        out_shape=(
+            jax.ShapeDtypeStruct((BLK, D), BF16),
+            jax.ShapeDtypeStruct((OUT, 2, COLS), BF16),
+        ),
+        in_specs=[vmem] * 2,
+        out_specs=(anywhere, anywhere),
+        scratch_shapes=[pltpu.SemaphoreType.DMA((2,))],
+    )(
+        pltpu.with_memory_space_constraint(state, pltpu.VMEM),
+        pltpu.with_memory_space_constraint(fields, pltpu.VMEM),
+    )
+    return state[None], fields[None]
 
 
 def solution(mesh):

time: 35.8 us -> 28.9 us (0.81)
  the two profiles are of different devices: /device:TPU:1 before, /device:TPU:224 now
where the time goes in v3:
time: 28.9 us; the launch traced here: 28.8 us
  Pallas kernels  28.1 us (97%)
  between operations  0.64 us (2%)
    pallas_call x1, Pallas kernels, shards(): pl.pallas_call(functools.partial(kernel, *sizes), out_shape=(pltpu.VMEM((...  27.4 us
    pallas_call x1, Pallas kernels, shards(): pl.pallas_call(store, out_shape=(jax.ShapeDtypeStruct((BLK, D), BF16), ja...  0.7 us

profile of v3, /device:TPU:224, one launch (start us, length us, event | category | flops | bytes accessed | tf_op | source)
XLA Modules:
  0.0 28.8 jit_solution(4877692115057768367)
XLA Ops:
  0.6 27.4 %shard_map.104 = (bf16[128,512]{1,0:T(8,128)(2,1)S(1)}, bf16[84,2,256]{2,1,0:T(2,128)(2,1)S(1)}) custom-call(bf16[128,512]{1,0:T(8,128)(2,1)} %bitcast.7, f32[1,512]{1,0:T(1,128)} %bitcast.9, bf16[512,1536]{1,0:T(8,128)(2,1)} %wqkv_h.1, bf16[512,512]{1,0:T(8,128)(2,1)} %wout_h.1, bf16[512,512]{1,0:T(8,128)(2,1)} %wlat_h.1, s32[1,5]{1,0:T(1,128)} %nbr_h.1, ...), custom_call_target="tpu_custom_call" | custom-call | tf_op jit(solution)/shard_map/pallas_call | solution.py:435
  28.1 0.7 %shard_map.105 = (bf16[128,512]{1,0:T(8,128)(2,1)}, bf16[84,2,256]{2,1,0:T(2,128)(2,1)}) custom-call(bf16[128,512]{1,0:T(8,128)(2,1)S(1)} %get-tuple-element.6.state, bf16[84,2,256]{2,1,0:T(2,128)(2,1)S(1)} %get-tuple-element.7.fields), custom_call_target="tpu_custom_call" | custom-call | tf_op jit(solution)/shard_map/pallas_call | solution.py:480

commit v4 on v3

--- a/solution.py
+++ b/solution.py
@@ -34,8 +34,8 @@
     nodes_h, gain_h, wqkv_h, wout_h, wlat_h, nbr_h, asg_h, psi_h, wdec_h,
     state_o, fields_o,
     xs, gain, wqkv, wout, wlat, nbr, asg, psi, psi_s, wdec, wtp,
-    slots, qb, kb, vb, att, lat, edge, edges_in, onehot_e,
-    hot, kron, hsel, splat, sel,
+    slots, qb, kb, vb, own_num, own_den, own_top, att, lat, edge, edges_in, onehot_e,
+    hot, kron, hsel, splat, sel, other,
     load_sem, send_sem, recv_sem,
 ):
     reg, lon = lax.axis_index("reg"), lax.axis_index("lon")
@@ -268,6 +268,34 @@
     keys_values(UP, 2)
     selections(2)
 
+    head_lane = iota((BLK, 128), 1) // 32
+    zero = jnp.zeros((BLK, 128), BF16)
+
+    def attend(part, keys, vals):
+        q = qb[:, part]
+        wide = jnp.concatenate([jnp.where(head_lane == h, q, zero) for h in range(4)], axis=0)
+        scores = lax.dot_general(wide, keys, NT, preferred_element_type=F32)
+        top = jnp.max(scores, axis=-1, keepdims=True)
+        weights = jnp.exp2(scores - top).astype(BF16)
+        ones = jnp.ones(vals.shape, BF16)
+        summed = jnp.dot(
+            weights, jnp.concatenate([vals, ones], axis=1), preferred_element_type=F32
+        )
+        num, den = summed[:BLK, :128], summed[:BLK, 128:]
+        most = jnp.broadcast_to(top[:BLK], (BLK, 128))
+        for h in range(1, 4):
+            mine, rows = head_lane == h, slice(h * BLK, (h + 1) * BLK)
+            num = jnp.where(mine, summed[rows, :128], num)
+            den = jnp.where(mine, summed[rows, 128:], den)
+            most = jnp.where(mine, top[rows], most)
+        return num, den, most
+
+    for g in range(4):
+        part = pl.ds(g * 128, 128)
+        own_num[:, part], own_den[:, part], own_top[:, part] = attend(
+            part, kb[CODE[OWN], :, part], vb[CODE[OWN], :, part]
+        )
+
     loads[6].wait()
     for o in range(OUTP // 16):
         for b in range(NBAS):
@@ -300,32 +328,22 @@
         keys_values(UL, 4, half * (BLK // 2), BLK // 2)
 
     slot = []
-    for n in range(5):
+    for n in range(1, 5):
         there = nbr[0, n]
         row_step = there // n_lon - reg
         col_step = lax.rem(there % n_lon - lon + 1 + n_lon, n_lon) - 1
         code = (row_step + 1) * 3 + col_step + 1
         slot.append(jnp.clip(code, 0, 8))
-    head_lane = lax.broadcasted_iota(jnp.int32, (BLK, 128), 1) // 32
-    ones = jnp.ones((5 * BLK, 128), BF16)
-    zero = jnp.zeros((BLK, 128), BF16)
     for g in range(4):
         part = pl.ds(g * 128, 128)
         keys = jnp.concatenate([kb[s, :, part] for s in slot], axis=0)
         vals = jnp.concatenate([vb[s, :, part] for s in slot], axis=0)
-        q = qb[:, part]
-        wide = jnp.concatenate([jnp.where(head_lane == h, q, zero) for h in range(4)], axis=0)
-        scores = lax.dot_general(wide, keys, NT, preferred_element_type=F32)
-        top = jnp.max(scores, axis=-1, keepdims=True)
-        weights = jnp.exp2(scores - top).astype(BF16)
-        summed = jnp.dot(
-            weights, jnp.concatenate([vals, ones], axis=1), preferred_element_type=F32
-        )
-        num, den = summed[:BLK, :128], summed[:BLK, 128:]
-        for h in range(1, 4):
-            mine = head_lane == h
-            num = jnp.where(mine, summed[h * BLK : (h + 1) * BLK, :128], num)
-            den = jnp.where(mine, summed[h * BLK : (h + 1) * BLK, 128:], den)
+        num, den, top = attend(part, keys, vals)
+        first = own_top[:, part]
+        both = jnp.maximum(first, top)
+        old, new = jnp.exp2(first - both), jnp.exp2(top - both)
+        num = num * new + own_num[:, part] * old
+        den = den * new + own_den[:, part] * old
         att[:, part] = (num / den).astype(BF16)
 
     loads[7].wait()
@@ -378,15 +396,21 @@
     total = decode_own()
 
     even = lax.rem(reg, 2) == 0
-    near, far = jnp.where(even, 1, 0), jnp.where(even, 0, 1)
-    remote(C_LUP + 1 - near, lat.at[1], lat.at[near * 2], up).wait_recv()
-    other = decode_far(mixed(lat[near * 2]), near)
     has_far = jnp.logical_or(jnp.logical_and(even, has_up), jnp.logical_and(reg % 2 == 1, has_down))
-
-    @pl.when(has_far)
-    def _():
-        remote(C_LUP + 1 - far, lat.at[1], lat.at[far * 2], up).wait_recv()
-
+    near = jnp.where(even, 1, 0)
+    other[...] = jnp.zeros((OUTP, 2 * COLS), F32)
+
+    def add_block(n, _):
+        k = jnp.where(n == 0, near, 1 - near)
+
+        @pl.when(jnp.logical_or(n == 0, has_far))
+        def _():
+            remote(C_LUP + 1 - k, lat.at[1], lat.at[k * 2], up).wait_recv()
+
+        other[...] += decode_far(mixed(lat[k * 2]), k)
+        return 0
+
+    lax.fori_loop(0, 2, add_block, 0)
     wait_all([C_EDGE, C_EDGE + 1])
     pl.when(has_down)(lambda: wait_all([C_EDGE + 2, C_EDGE + 3]))
     pl.when(has_up)(lambda: wait_all([C_EDGE + 4, C_EDGE + 5]))
@@ -395,9 +419,7 @@
     for n in range(3):
         a, b = edges_in[2 * n], edges_in[2 * n + 1]
         cells.append(jnp.where(first4, a, b))
-    z = mixed(jnp.concatenate([lat[far * 2]] + cells + [jnp.zeros((80, D), BF16)], axis=0))
-    other += decode_far(z[:, :BLK], far)
-    z = by_output(z[:, BLK:])
+    z = by_output(mixed(jnp.concatenate(cells + [jnp.zeros((80, D), BF16)], axis=0)))
     sides = lax.dot_general(z, hsel[...], NT, preferred_element_type=F32)
     sides = jnp.concatenate([sides, jnp.zeros((OUTP, 112), F32)], axis=1)
     lane2 = iota((OUTP, 128), 1)
@@ -456,6 +478,9 @@
             pltpu.VMEM((BLK, D), BF16),
             pltpu.VMEM((9, BLK, D), BF16),
             pltpu.VMEM((9, BLK, D), BF16),
+            pltpu.VMEM((BLK, D), F32),
+            pltpu.VMEM((BLK, D), F32),
+            pltpu.VMEM((BLK, D), F32),
             pltpu.VMEM((BLK, D), BF16),
             pltpu.VMEM((3, BLK, D), BF16),
             pltpu.VMEM((16, D), BF16),
@@ -466,6 +491,7 @@
             pltpu.VMEM((16, NBAS * 128), BF16),
             pltpu.VMEM((30 * NBAS, 16, 128), BF16),
             pltpu.VMEM((2, NBAS * BLK, 2 * COLS), BF16),
+            pltpu.VMEM((OUTP, 2 * COLS), F32),
             pltpu.SemaphoreType.DMA((10,)),
             pltpu.SemaphoreType.DMA((N_COPIES,)),
             pltpu.SemaphoreType.DMA((N_COPIES,)),

time: 28.9 us -> 28.1 us (0.972)
  the two profiles are of different devices: /device:TPU:224 before, /device:TPU:1 now
where the time goes in v4:
time: 28.1 us; the launch traced here: 27.6 us
  Pallas kernels  27 us (96%)
  between operations  0.64 us (2%)
    pallas_call x1, Pallas kernels, shards(): pl.pallas_call(functools.partial(kernel, *sizes), out_shape=(pltpu.VMEM((...  26.3 us
    pallas_call x1, Pallas kernels, shards(): pl.pallas_call(store, out_shape=(jax.ShapeDtypeStruct((BLK, D), BF16), ja...  0.7 us

profile of v4, /device:TPU:1, one launch (start us, length us, event | category | flops | bytes accessed | tf_op | source)
XLA Modules:
  0.0 27.6 jit_solution(18241863832102746696)
XLA Ops:
  0.6 26.3 %shard_map.104 = (bf16[128,512]{1,0:T(8,128)(2,1)S(1)}, bf16[84,2,256]{2,1,0:T(2,128)(2,1)S(1)}) custom-call(bf16[128,512]{1,0:T(8,128)(2,1)} %bitcast.7, f32[1,512]{1,0:T(1,128)} %bitcast.9, bf16[512,1536]{1,0:T(8,128)(2,1)} %wqkv_h.1, bf16[512,512]{1,0:T(8,128)(2,1)} %wout_h.1, bf16[512,512]{1,0:T(8,128)(2,1)} %wlat_h.1, s32[1,5]{1,0:T(1,128)} %nbr_h.1, ...), custom_call_target="tpu_custom_call" | custom-call | tf_op jit(solution)/shard_map/pallas_call | solution.py:457
  26.9 0.7 %shard_map.105 = (bf16[128,512]{1,0:T(8,128)(2,1)}, bf16[84,2,256]{2,1,0:T(2,128)(2,1)}) custom-call(bf16[128,512]{1,0:T(8,128)(2,1)S(1)} %get-tuple-element.6.state, bf16[84,2,256]{2,1,0:T(2,128)(2,1)S(1)} %get-tuple-element.7.fields), custom_call_target="tpu_custom_call" | custom-call | tf_op jit(solution)/shard_map/pallas_call | solution.py:506

commit v5 on v4

--- a/solution.py
+++ b/solution.py
@@ -318,14 +318,13 @@
     hits = jnp.where(node[:, :128] == tall, 1.0, 0.0)
     onehot_e[...] = jnp.transpose(hits)[:16].astype(BF16)
 
-    for half in range(2):
-        chunks = range(half * CHUNKS // 2, (half + 1) * CHUNKS // 2)
+    for chunks in (range(CHUNKS - 1), range(CHUNKS - 1, CHUNKS)):
         from_down, from_up = (
             [C_DIAG + 4 * c + 2 * side + v for c in chunks for side in (0, 1)] for v in (0, 1)
         )
         pl.when(has_down)(lambda keys=from_down: wait_all(keys))
         pl.when(has_up)(lambda keys=from_up: wait_all(keys))
-        keys_values(UL, 4, half * (BLK // 2), BLK // 2)
+        keys_values(UL, 4, chunks[0] * rows, len(chunks) * rows)
 
     slot = []
     for n in range(1, 5):
@@ -360,9 +359,11 @@
         copies[C_EDGE + n] = remote(C_EDGE + n, edge, edges_in.at[there], to)
     copies[C_LUP] = remote(C_LUP, lat.at[1], lat.at[2], up)
     copies[C_LDOWN] = remote(C_LDOWN, lat.at[1], lat.at[0], down)
+    pl.when(has_up)(lambda: start_all([C_EDGE + 2, C_EDGE + 3]))
+    pl.when(has_down)(lambda: start_all([C_EDGE + 4, C_EDGE + 5]))
     start_all([C_EDGE, C_EDGE + 1])
-    pl.when(has_up)(lambda: start_all([C_EDGE + 2, C_EDGE + 3, C_LUP]))
-    pl.when(has_down)(lambda: start_all([C_EDGE + 4, C_EDGE + 5, C_LDOWN]))
+    pl.when(has_up)(lambda: start_all([C_LUP]))
+    pl.when(has_down)(lambda: start_all([C_LDOWN]))
     upward.extend([C_EDGE + 2, C_EDGE + 3, C_LUP])
     downward.extend([C_EDGE + 4, C_EDGE + 5, C_LDOWN])
 

time: 28.1 us -> 28.3 us (level)
  no operation moved by 1% of the time
where the time goes in v5:
time: 28.3 us; the launch traced here: 27.8 us
  Pallas kernels  27.1 us (96%)
  between operations  0.64 us (2%)
    pallas_call x1, Pallas kernels, shards(): pl.pallas_call(functools.partial(kernel, *sizes), out_shape=(pltpu.VMEM((...  26.4 us
    pallas_call x1, Pallas kernels, shards(): pl.pallas_call(store, out_shape=(jax.ShapeDtypeStruct((BLK, D), BF16), ja...  0.7 us

profile of v5, /device:TPU:1, one launch (start us, length us, event | category | flops | bytes accessed | tf_op | source)
XLA Modules:
  0.0 27.8 jit_solution(3525691028395399681)
XLA Ops:
  0.6 26.4 %shard_map.104 = (bf16[128,512]{1,0:T(8,128)(2,1)S(1)}, bf16[84,2,256]{2,1,0:T(2,128)(2,1)S(1)}) custom-call(bf16[128,512]{1,0:T(8,128)(2,1)} %bitcast.7, f32[1,512]{1,0:T(1,128)} %bitcast.9, bf16[512,1536]{1,0:T(8,128)(2,1)} %wqkv_h.1, bf16[512,512]{1,0:T(8,128)(2,1)} %wout_h.1, bf16[512,512]{1,0:T(8,128)(2,1)} %wlat_h.1, s32[1,5]{1,0:T(1,128)} %nbr_h.1, ...), custom_call_target="tpu_custom_call" | custom-call | tf_op jit(solution)/shard_map/pallas_call | solution.py:458
  27.1 0.7 %shard_map.105 = (bf16[128,512]{1,0:T(8,128)(2,1)}, bf16[84,2,256]{2,1,0:T(2,128)(2,1)}) custom-call(bf16[128,512]{1,0:T(8,128)(2,1)S(1)} %get-tuple-element.6.state, bf16[84,2,256]{2,1,0:T(2,128)(2,1)S(1)} %get-tuple-element.7.fields), custom_call_target="tpu_custom_call" | custom-call | tf_op jit(solution)/shard_map/pallas_call | solution.py:507

commit v6 on v4

--- a/solution.py
+++ b/solution.py
@@ -11,7 +11,7 @@
 MESH = pl.DeviceIdType.MESH
 F32, BF16 = jnp.float32, jnp.bfloat16
 HEADS = 16
-CHUNKS = 4
+CHUNKS = 2
 BLK, D = 128, 512
 COLS = 256
 NBAS, OUT, OUTP = 9, 84, 96
@@ -259,13 +259,11 @@
     pl.when(has_up)(lambda: wait_all([C_ADOWN]))
     one_hots(0)
     one_hots(2)
-    relay(2)
-    selections(0)
-    relay(3)
     keys_values(LEFT, 2)
     pl.when(has_down)(lambda: wait_all([C_UP]))
     pl.when(has_up)(lambda: wait_all([C_DOWN]))
     keys_values(UP, 2)
+    selections(0)
     selections(2)
 
     head_lane = iota((BLK, 128), 1) // 32

time: 28.1 us -> 28.3 us (level)
  no operation moved by 1% of the time
where the time goes in v6:
time: 28.3 us; the launch traced here: 27.8 us
  Pallas kernels  27.2 us (96%)
  between operations  0.64 us (2%)
    pallas_call x1, Pallas kernels, shards(): pl.pallas_call(functools.partial(kernel, *sizes), out_shape=(pltpu.VMEM((...  26.5 us
    pallas_call x1, Pallas kernels, shards(): pl.pallas_call(store, out_shape=(jax.ShapeDtypeStruct((BLK, D), BF16), ja...  0.7 us

profile of v6, /device:TPU:1, one launch (start us, length us, event | category | flops | bytes accessed | tf_op | source)
XLA Modules:
  0.0 27.8 jit_solution(14350493848026046194)
XLA Ops:
  0.6 26.5 %shard_map.104 = (bf16[128,512]{1,0:T(8,128)(2,1)S(1)}, bf16[84,2,256]{2,1,0:T(2,128)(2,1)S(1)}) custom-call(bf16[128,512]{1,0:T(8,128)(2,1)} %bitcast.7, f32[1,512]{1,0:T(1,128)} %bitcast.9, bf16[512,1536]{1,0:T(8,128)(2,1)} %wqkv_h.1, bf16[512,512]{1,0:T(8,128)(2,1)} %wout_h.1, bf16[512,512]{1,0:T(8,128)(2,1)} %wlat_h.1, s32[1,5]{1,0:T(1,128)} %nbr_h.1, ...), custom_call_target="tpu_custom_call" | custom-call | tf_op jit(solution)/shard_map/pallas_call | solution.py:455
  27.1 0.7 %shard_map.105 = (bf16[128,512]{1,0:T(8,128)(2,1)}, bf16[84,2,256]{2,1,0:T(2,128)(2,1)}) custom-call(bf16[128,512]{1,0:T(8,128)(2,1)S(1)} %get-tuple-element.6.state, bf16[84,2,256]{2,1,0:T(2,128)(2,1)S(1)} %get-tuple-element.7.fields), custom_call_target="tpu_custom_call" | custom-call | tf_op jit(solution)/shard_map/pallas_call | solution.py:504
